TPU v7x, 32 devices: a whole 2x2x4 slice. The times are simulated.
32 devices in a mesh: parts: 2 (over y), blk: 4 (over z), grp: 2 (over x), fld: 2 (over core).
Axes of the slice: x: 2, y: 2, z: 4, core: 2. Of those that a mesh axis runs over, the one named last changes fastest.
Arguments:
- coords: float32 [32, 2, 2, 128], P(('parts', 'blk'), 'grp'), parts along dimension 0, may hold values from 0 to 1
- fields: float32 [32, 2, 64, 128], P(('parts', 'blk'), 'grp', 'fld'), parts along dimension 0, may hold values from -6 to 6
- neighbours: int32 [32, 2, 4], P(('parts', 'blk'), 'grp'), parts along dimension 0, may hold values from -1 to 29, as said below
Outputs:
- whitened: float32 [32, 2, 64, 128], P(('parts', 'blk'), 'grp', 'fld'), parts along dimension 0
- precision_product: float32 [32, 2, 64, 128], P(('parts', 'blk'), 'grp', 'fld'), parts along dimension 0
There are 2 independent parts, one for each index of `parts`. A program takes and returns all parts, laid end to end along the dimension named above; each array names one. Nothing has to cross between parts.
Inputs may be any that keep to these rules, and one draw needn't show every extreme that they name: `neighbours`: each entry is -1 or the flat id j * 2 + h of a block with i - 8 <= j <= i - 1 and |h - g| <= 1, where (i, g) is the listing block; the ids of one list differ.
All inputs are finite; a program needn't handle non-finite values.
Results may differ from a plain program's by a relative error of at most 0.0003.
Values sent between devices are 32-bit elements; how exact they have to be, the bound alone decides.
A program may use at most 64 MiB of HBM per device.

v0:
```python
import jax
import jax.numpy as jnp
from jax import lax
from jax.sharding import PartitionSpec as P

ELL = 0.3
NUGGET = 0.25


def padded_2(cells, sides, width):
    for axis, dim in sides:
        count = lax.axis_size(axis)
        ends = count - 1
        head = lax.slice_in_dim(cells, 0, width, axis=dim)
        tail = lax.slice_in_dim(cells, cells.shape[dim] - width, cells.shape[dim], axis=dim)
        cells = jnp.concatenate(
            [
                lax.ppermute(tail, axis, [(i, (i + 1) % count) for i in range(ends)]),
                cells,
                lax.ppermute(head, axis, [((i + 1) % count, i) for i in range(ends)]),
            ],
            axis=dim,
        )
    return cells


def shifted(block, axis, distance):
    devices = range(lax.axis_size(axis))
    route = [(i - distance, i) for i in devices if i - distance in devices]
    return lax.ppermute(block, axis, route)


def one_block(pts, vals, mask):
    count = pts.shape[0] * pts.shape[2]
    points = jnp.transpose(pts, (0, 2, 1)).reshape(count, 2)
    mpts = jnp.repeat(mask, pts.shape[2])
    delta_x = points[:, 0][:, None] - points[:, 0][None, :]
    delta_y = points[:, 1][:, None] - points[:, 1][None, :]
    scaled = jnp.sqrt(3.0) * jnp.sqrt(delta_x * delta_x + delta_y * delta_y) / ELL
    kernel = (1.0 + scaled) * jnp.exp(-scaled)
    cov = mpts[:, None] * mpts[None, :] * kernel + jnp.diag(NUGGET * mpts + 1.0 - mpts)
    factor = jnp.linalg.cholesky(cov)
    values = jnp.transpose(vals, (0, 2, 1)).reshape(count, vals.shape[1]) * mpts[:, None]
    solved = jax.scipy.linalg.solve_triangular(factor, values, lower=True)
    mine = solved[count - pts.shape[2] :]
    padded = jnp.concatenate(
        [jnp.zeros((count - pts.shape[2], vals.shape[1]), jnp.float32), mine], axis=0
    )
    back = jax.scipy.linalg.solve_triangular(factor, padded, lower=True, trans="T") * mpts[:, None]
    back = jnp.transpose(back.reshape(pts.shape[0], pts.shape[2], vals.shape[1]), (0, 2, 1))
    return (mine.T, back)


def fetch_across(local):
    return padded_2(local, (("grp", 1),), 1)


def fetch_older(local):
    older = []
    for distance in (2, 1):
        older.append(shifted(local, "blk", distance))
    return jnp.concatenate(older + [local], axis=0)


def back_across(terms):
    total_count = terms[:, 1:2]
    for column, offset in ((0, -1), (2, 1)):
        total_count = total_count + shifted(terms[:, column : column + 1], "grp", offset)
    return total_count


def back_older(terms):
    per = terms.shape[0] // 3
    farthest = terms[:per]
    nearest = terms[per : 2 * per]
    total_count = terms[2 * per :]
    for distance, piece in ((1, nearest), (2, farthest)):
        total_count = total_count + shifted(piece, "blk", -distance)
    return total_count


def per_device(coords, fields, neighbours):
    per = coords.shape[0]
    local_fields = fields.shape[2]
    points = coords.shape[3]
    local = jnp.concatenate([coords, fields], axis=2)
    window = fetch_older(fetch_across(local))
    groups = lax.axis_size("grp")
    blk_pos = lax.axis_index("blk")
    grp_pos = lax.axis_index("grp")
    neighbour_lists = neighbours.reshape(per, neighbours.shape[2])
    earlier = neighbour_lists // groups - (blk_pos - 2) * per
    beside = neighbour_lists % groups - grp_pos + 1
    own_slot = ((2 * per + jnp.arange(per, dtype=jnp.int32)) * 3 + 1)[:, None]
    slots = jnp.concatenate(
        [jnp.where(neighbour_lists >= 0, earlier * 3 + beside, own_slot), own_slot], axis=1
    )
    masks = jnp.concatenate(
        [(neighbour_lists >= 0).astype(jnp.float32), jnp.ones((per, 1), jnp.float32)], axis=1
    )
    flat_window = window.reshape(9 * per, 2 + local_fields, points)
    width = slots.shape[1]
    all_fields = lax.all_gather(flat_window[:, 2:], "fld", axis=1, tiled=True)
    full_window = jnp.concatenate([flat_window[:, :2], all_fields], axis=1)
    half = per // lax.axis_size("fld")
    first = lax.axis_index("fld") * half
    my_slots = lax.dynamic_slice_in_dim(slots, first, half, 0)
    my_masks = lax.dynamic_slice_in_dim(masks, first, half, 0)

    def visit_mine(index):
        rows = full_window[my_slots[index]]
        return one_block(rows[:, :2], rows[:, 2:], my_masks[index])

    mine_white, mine_backs = lax.map(visit_mine, jnp.arange(half, dtype=jnp.int32))
    whitened, backs = (
        lax.all_to_all(mine_white[:, None], "fld", split_axis=2, concat_axis=0, tiled=True),
        lax.all_to_all(mine_backs, "fld", split_axis=2, concat_axis=0, tiled=True),
    )
    whitened = whitened[:, 0]
    onehot = (slots.reshape(-1)[None, :] == jnp.arange(9 * per, dtype=jnp.int32)[:, None]).astype(
        jnp.float32
    )
    onehot = onehot * masks.reshape(-1)[None, :]
    terms = jnp.dot(
        onehot, backs.reshape(width * per, local_fields * points), precision=lax.Precision.HIGHEST
    )
    terms = terms.reshape(3 * per, 3, local_fields, points)
    product = back_across(back_older(terms))
    return (whitened[:, None], product)


def solution(mesh):
    return jax.shard_map(
        per_device,
        mesh=mesh,
        in_specs=(
            P(("parts", "blk"), "grp", None, None),
            P(("parts", "blk"), "grp", "fld", None),
            P(("parts", "blk"), "grp", None),
        ),
        out_specs=(
            P(("parts", "blk"), "grp", "fld", None),
            P(("parts", "blk"), "grp", "fld", None),
        ),
        check_vma=False,
    )
```

profile of v0, /device:TPU:0, one launch (start us, length us, event | category | flops | bytes accessed | tf_op | source)
XLA Modules:
  0.0 478.8 jit_solution(597964781460858947)
XLA Ops:
  8.1 4.8 %collective-permute-start = (f32[4,1,34,128]{3,2,1,0:T(8,128)S(1)}, f32[4,1,34,128]{3,2,1,0:T(8,128)S(1)}, u32[]{:S(2)}, u32[]{:S(2)}) collective-permute-start(f32[4,1,34,128]{3,2,1,0:T(8,128)S(1)} %pad_maximum_fusion.2), channel_id=1, source_target_pairs={{0,2},{1,3},{4,6},{5,7},{8,10},{9,11},{12,14},{13,15},{16,18},{17,... | collective-permute-start | bytes 208904 | tf_op jit(solution)/shard_map/ppermute | solution.py:18
  12.9 1.3 collective-permute-start.1
  15.0 4.3 collective-permute-done.1
  20.1 4.5 collective-permute-start.2
  24.6 3.5 collective-permute-start.3
  28.2 2.4 collective-permute-done.2
  30.6 3.1 collective-permute-done.3
  36.0 14.3 %all-gather.2.cloned.1.call-done = f32[36,64,128]{2,1,0:T(8,128)} async-done(((f32[36,32,128]{2,1,0:T(8,128)}), f32[36,64,128]{2,1,0:T(8,128)}) %all-gather.2.cloned.1.call-update) | async-done | bytes 1179664 | tf_op jit(solution)/shard_map/all_gather | solution.py:103
  50.3 2.4 pad_maximum_fusion
  53.3 382.8 %while.17 = (s32[]{:T(128)}, f32[2,64,128]{2,0,1:T(2,128)}, f32[2,5,64,128]{3,0,1,2:T(2,128)}, s32[2]{0:T(128)}, f32[2,5]{1,0:T(2,128)S(1)}, /*index=5*/s32[2,5]...) while((s32[]{:T(128)}, f32[2,64,128]{2,0,1:T(2,128)}, ...), condition=%wide.region_11.12_spmd, body=%wide.region_0.11_spmd.sunk | while | flops 1146998272 | bytes 28961552 | solution.py:114
  56.5 1.9 gather_fusion
  58.6 2.3 fusion.201
  60.9 11.7 %cholesky.540 = f32[128,128]{1,0:T(8,128)S(1)} custom-call(f32[128,128]{1,0:T(8,128)S(1)} %cholesky.539), custom_call_target="Cholesky" | custom-call | tf_op jit(solution)/shard_map/while/body/eval_jaxpr/jit(cholesky)/cholesky | solution.py:42
  72.7 10.4 %custom-call.89 = f32[1,128,128]{1,2,0:T(8,128)} custom-call(f32[1,128,128]{2,1,0:T(8,128)S(1)} %get-tuple-element.246), custom_call_target="InvertDiagBlocksLowerTriangular" | custom-call | tf_op jit(solution)/shard_map/while/body/eval_jaxpr/jit(cholesky)/cholesky | solution.py:42
  84.3 1.3 convolution_subtract_fusion.24
  85.7 12.3 %cholesky.543 = f32[128,128]{1,0:T(8,128)S(1)} custom-call(f32[128,128]{1,0:T(8,128)S(1)} %cholesky.542), custom_call_target="Cholesky" | custom-call | tf_op jit(solution)/shard_map/while/body/eval_jaxpr/jit(cholesky)/cholesky | solution.py:42
  99.8 9.8 %custom-call.90 = f32[1,128,128]{1,2,0:T(8,128)S(1)} custom-call(f32[1,128,128]{2,1,0:T(8,128)S(1)} %get-tuple-element.250), custom_call_target="InvertDiagBlocksLowerTriangular" | custom-call | tf_op jit(solution)/shard_map/while/body/eval_jaxpr/jit(cholesky)/cholesky | solution.py:42
  110.0 1.4 convolution_subtract_fusion.25
  111.4 11.7 %cholesky.545 = f32[128,128]{1,0:T(8,128)S(1)} custom-call(f32[128,128]{1,0:T(8,128)S(1)} %cholesky.544), custom_call_target="Cholesky" | custom-call | tf_op jit(solution)/shard_map/while/body/eval_jaxpr/jit(cholesky)/cholesky | solution.py:42
  124.4 9.8 %custom-call.91 = f32[1,128,128]{1,2,0:T(8,128)S(1)} custom-call(f32[1,128,128]{2,1,0:T(8,128)S(1)} %get-tuple-element.252), custom_call_target="InvertDiagBlocksLowerTriangular" | custom-call | tf_op jit(solution)/shard_map/while/body/eval_jaxpr/jit(cholesky)/cholesky | solution.py:42
  134.5 1.4 convolution_subtract_fusion.26
  135.9 11.9 %cholesky.547 = f32[128,128]{1,0:T(8,128)S(1)} custom-call(f32[128,128]{1,0:T(8,128)S(1)} %cholesky.546), custom_call_target="Cholesky" | custom-call | tf_op jit(solution)/shard_map/while/body/eval_jaxpr/jit(cholesky)/cholesky | solution.py:42
  149.1 9.8 %custom-call.92 = f32[1,128,128]{1,2,0:T(8,128)S(1)} custom-call(f32[1,128,128]{2,1,0:T(8,128)S(1)} %get-tuple-element.254), custom_call_target="InvertDiagBlocksLowerTriangular" | custom-call | tf_op jit(solution)/shard_map/while/body/eval_jaxpr/jit(cholesky)/cholesky | solution.py:42
  159.1 1.2 convolution_subtract_fusion.27
  160.4 11.7 %cholesky.548 = f32[128,128]{1,0:T(8,128)S(1)} custom-call(f32[128,128]{1,0:T(8,128)S(1)} %convolution_subtract_fusion.27), custom_call_target="Cholesky" | custom-call | tf_op jit(solution)/shard_map/while/body/eval_jaxpr/jit(cholesky)/cholesky | solution.py:42
  173.6 10.4 %while.18 = (s32[]{:T(128)}, f32[640,640]{1,0:T(8,128)S(1)}, s32[5,2]{0,1:T(2,128)S(1)}, f32[5,128,128]{2,1,0:T(8,128)S(1)}, s32[]{:T(128)}) while((s32[]{:T(128)}, f32[640,640]{1,0:T(8,128)S(1)}, s32[5,2]{0,1:T(2,128)S(1)}, f32[5,128,128]{2,1,0:T(8,128)S(1)}, s32[]{:T(128)}) %tuple.78), condition=%wide.while_cond, body=%wide.while_body.sunk | while | flops 2 | bytes 131181 | solution.py:44
  174.5 1.3 bitcast_dynamic-update-slice_fusion.2
  176.5 1.3 bitcast_dynamic-update-slice_fusion.2
  178.5 1.3 bitcast_dynamic-update-slice_fusion.2
  180.6 1.3 bitcast_dynamic-update-slice_fusion.2
  182.6 1.3 bitcast_dynamic-update-slice_fusion.2
  183.9 49.1 %custom-call.94 = f32[5,128,128]{1,2,0:T(8,128)S(1)} custom-call(f32[5,128,128]{2,1,0:T(8,128)S(1)} %get-tuple-element.263), custom_call_target="InvertDiagBlocksLowerTriangular" | custom-call | tf_op jit(solution)/shard_map/while/body/eval_jaxpr/jit(_solve_triangular)/triangular_solve | solution.py:44
  238.0 4.7 dynamic_update_slice.17
  247.1 1.9 gather_fusion
  249.2 2.3 fusion.201
  251.5 11.7 %cholesky.540 = f32[128,128]{1,0:T(8,128)S(1)} custom-call(f32[128,128]{1,0:T(8,128)S(1)} %cholesky.539), custom_call_target="Cholesky" | custom-call | tf_op jit(solution)/shard_map/while/body/eval_jaxpr/jit(cholesky)/cholesky | solution.py:42
  263.3 10.4 %custom-call.89 = f32[1,128,128]{1,2,0:T(8,128)} custom-call(f32[1,128,128]{2,1,0:T(8,128)S(1)} %get-tuple-element.246), custom_call_target="InvertDiagBlocksLowerTriangular" | custom-call | tf_op jit(solution)/shard_map/while/body/eval_jaxpr/jit(cholesky)/cholesky | solution.py:42
  274.9 1.3 convolution_subtract_fusion.24
  276.3 11.9 %cholesky.543 = f32[128,128]{1,0:T(8,128)S(1)} custom-call(f32[128,128]{1,0:T(8,128)S(1)} %cholesky.542), custom_call_target="Cholesky" | custom-call | tf_op jit(solution)/shard_map/while/body/eval_jaxpr/jit(cholesky)/cholesky | solution.py:42
  290.0 9.8 %custom-call.90 = f32[1,128,128]{1,2,0:T(8,128)S(1)} custom-call(f32[1,128,128]{2,1,0:T(8,128)S(1)} %get-tuple-element.250), custom_call_target="InvertDiagBlocksLowerTriangular" | custom-call | tf_op jit(solution)/shard_map/while/body/eval_jaxpr/jit(cholesky)/cholesky | solution.py:42
  300.2 1.4 convolution_subtract_fusion.25
  301.6 11.7 %cholesky.545 = f32[128,128]{1,0:T(8,128)S(1)} custom-call(f32[128,128]{1,0:T(8,128)S(1)} %cholesky.544), custom_call_target="Cholesky" | custom-call | tf_op jit(solution)/shard_map/while/body/eval_jaxpr/jit(cholesky)/cholesky | solution.py:42
  314.6 9.8 %custom-call.91 = f32[1,128,128]{1,2,0:T(8,128)S(1)} custom-call(f32[1,128,128]{2,1,0:T(8,128)S(1)} %get-tuple-element.252), custom_call_target="InvertDiagBlocksLowerTriangular" | custom-call | tf_op jit(solution)/shard_map/while/body/eval_jaxpr/jit(cholesky)/cholesky | solution.py:42
  324.7 1.4 convolution_subtract_fusion.26
  326.1 11.9 %cholesky.547 = f32[128,128]{1,0:T(8,128)S(1)} custom-call(f32[128,128]{1,0:T(8,128)S(1)} %cholesky.546), custom_call_target="Cholesky" | custom-call | tf_op jit(solution)/shard_map/while/body/eval_jaxpr/jit(cholesky)/cholesky | solution.py:42
  339.3 9.8 %custom-call.92 = f32[1,128,128]{1,2,0:T(8,128)S(1)} custom-call(f32[1,128,128]{2,1,0:T(8,128)S(1)} %get-tuple-element.254), custom_call_target="InvertDiagBlocksLowerTriangular" | custom-call | tf_op jit(solution)/shard_map/while/body/eval_jaxpr/jit(cholesky)/cholesky | solution.py:42
  349.4 1.2 convolution_subtract_fusion.27
  350.6 11.7 %cholesky.548 = f32[128,128]{1,0:T(8,128)S(1)} custom-call(f32[128,128]{1,0:T(8,128)S(1)} %convolution_subtract_fusion.27), custom_call_target="Cholesky" | custom-call | tf_op jit(solution)/shard_map/while/body/eval_jaxpr/jit(cholesky)/cholesky | solution.py:42
  363.8 10.6 %while.18 = (s32[]{:T(128)}, f32[640,640]{1,0:T(8,128)S(1)}, s32[5,2]{0,1:T(2,128)S(1)}, f32[5,128,128]{2,1,0:T(8,128)S(1)}, s32[]{:T(128)}) while((s32[]{:T(128)}, f32[640,640]{1,0:T(8,128)S(1)}, s32[5,2]{0,1:T(2,128)S(1)}, f32[5,128,128]{2,1,0:T(8,128)S(1)}, s32[]{:T(128)}) %tuple.78), condition=%wide.while_cond, body=%wide.while_body.sunk | while | flops 2 | bytes 131181 | solution.py:44
  364.9 1.3 bitcast_dynamic-update-slice_fusion.2
  366.9 1.3 bitcast_dynamic-update-slice_fusion.2
  369.0 1.3 bitcast_dynamic-update-slice_fusion.2
  371.0 1.3 bitcast_dynamic-update-slice_fusion.2
  373.0 1.3 bitcast_dynamic-update-slice_fusion.2
  374.4 49.1 %custom-call.94 = f32[5,128,128]{1,2,0:T(8,128)S(1)} custom-call(f32[5,128,128]{2,1,0:T(8,128)S(1)} %get-tuple-element.263), custom_call_target="InvertDiagBlocksLowerTriangular" | custom-call | tf_op jit(solution)/shard_map/while/body/eval_jaxpr/jit(_solve_triangular)/triangular_solve | solution.py:44
  428.4 4.7 dynamic_update_slice.17
  436.1 5.1 %all_to_all.33 = f32[2,5,64,128]{3,0,1,2:T(2,128)S(1)} all-to-all(f32[2,5,64,128]{3,0,1,2:T(2,128)} %get-tuple-element.93), channel_id=1, replica_groups=mesh['parts'=2,'blk'=4,'grp'=2,'fld'=2] {'fld'}, dimensions={2} | all-to-all | bytes 655360 | tf_op jit(solution)/shard_map/all_to_all | solution.py:117
  442.3 1.3 collective-permute-start.4
  443.7 1.3 collective-permute-start.5
  445.0 6.1 %collective-permute-done.4 = f32[4,3,32,128]{3,2,1,0:T(8,128)S(1)} collective-permute-done((f32[4,3,32,128]{3,2,1,0:T(8,128)S(1)}, f32[4,3,32,128]{3,2,1,0:T(8,128)S(1)}, u32[]{:S(2)}, u32[]{:S(2)}) %collective-permute-start.4) | collective-permute-done | bytes 196640 | tf_op jit(solution)/shard_map/ppermute | solution.py:30
  451.1 9.6 %collective-permute-done.5 = f32[4,3,32,128]{3,2,1,0:T(8,128)S(1)} collective-permute-done((f32[4,3,32,128]{3,2,1,0:T(8,128)S(1)}, f32[4,3,32,128]{3,2,1,0:T(8,128)S(1)}, u32[]{:S(2)}, u32[]{:S(2)}) %collective-permute-start.5) | collective-permute-done | bytes 196640 | tf_op jit(solution)/shard_map/ppermute | solution.py:30
  460.8 1.3 collective-permute-start.6
  462.1 4.5 collective-permute-start.7
  466.7 3.8 all_to_all.34
  (200 shorter events, 38.1 us)
Async XLA Ops:
  7.2 43.2 %all-gather.2.cloned.1.call-start = ((), (), s32[]{:S(2)}) async-start(), calls=%async_computation.2 | async-start | bytes 1769472 | tf_op jit(solution)/shard_map/all_gather | solution.py:103
  8.1 6.9 %collective-permute-start = (f32[4,1,34,128]{3,2,1,0:T(8,128)S(1)}, f32[4,1,34,128]{3,2,1,0:T(8,128)S(1)}, u32[]{:S(2)}, u32[]{:S(2)}) collective-permute-start(f32[4,1,34,128]{3,2,1,0:T(8,128)S(1)} %pad_maximum_fusion.2), channel_id=1, source_target_pairs={{0,2},{1,3},{4,6},{5,7},{8,10},{9,11},{12,14},{13,15},{16,18},{17,... | collective-permute-start | bytes 208904 | tf_op jit(solution)/shard_map/ppermute | solution.py:18
  12.9 6.3 %collective-permute-start.1 = (f32[4,1,34,128]{3,2,1,0:T(8,128)S(1)}, f32[4,1,34,128]{3,2,1,0:T(8,128)S(1)}, u32[]{:S(2)}, u32[]{:S(2)}) collective-permute-start(f32[4,1,34,128]{3,2,1,0:T(8,128)S(1)} %pad_maximum_fusion.2), channel_id=1, source_target_pairs={{2,0},{3,1},{6,4},{7,5},{10,8},{11,9},{14,12},{15,13},{18,16},{19,... | collective-permute-start | bytes 208904 | tf_op jit(solution)/shard_map/ppermute | solution.py:20
  20.1 15.5 %copy-start.7 = (s32[4,1,4]{2,1,0:T(1,128)S(1)}, s32[4,1,4]{2,1,0:T(1,128)}, u32[]{:S(2)}) copy-start(s32[4,1,4]{2,1,0:T(1,128)} %param.7) | copy-start | bytes 196
  20.1 10.4 %collective-permute-start.2 = (f32[4,3,34,128]{3,2,1,0:T(8,128)S(1)}, f32[4,3,34,128]{3,2,1,0:T(8,128)S(1)}, u32[]{:S(2)}, u32[]{:S(2)}) collective-permute-start(f32[4,3,34,128]{3,2,1,0:T(8,128)S(1)} %pad_maximum_fusion.1), channel_id=1, source_target_pairs={{0,8},{4,12},{1,9},{5,13},{2,10},{6,14},{3,11},{7,15},{16,24},{20,... | collective-permute-start | bytes 626696 | tf_op jit(solution)/shard_map/ppermute | solution.py:30
  24.6 9.1 %collective-permute-start.3 = (f32[4,3,34,128]{3,2,1,0:T(8,128)S(1)}, f32[4,3,34,128]{3,2,1,0:T(8,128)S(1)}, u32[]{:S(2)}, u32[]{:S(2)}) collective-permute-start(f32[4,3,34,128]{3,2,1,0:T(8,128)S(1)} %pad_maximum_fusion.1), channel_id=1, source_target_pairs={{0,4},{4,8},{8,12},{1,5},{5,9},{9,13},{2,6},{6,10},{10,14},{3,7},{... | collective-permute-start | bytes 626696 | tf_op jit(solution)/shard_map/ppermute | solution.py:30
  60.9 23.4 %copy-start = (f32[640,640]{1,0:T(8,128)}, f32[640,640]{1,0:T(8,128)S(1)}, u32[]{:S(2)}) copy-start(f32[640,640]{1,0:T(8,128)S(1)} %fusion.201) | copy-start | bytes 4915204 | tf_op jit(solution)/shard_map/while
  83.1 0.8 copy-start.1
  235.6 2.4 copy-start.2
  236.1 6.6 %copy-start.4 = (f32[2,64,128]{2,0,1:T(2,128)S(1)}, f32[2,64,128]{2,0,1:T(2,128)}, u32[]{:S(2)}) copy-start(f32[2,64,128]{2,0,1:T(2,128)} %get-tuple-element.299) | copy-start | bytes 196612 | tf_op jit(solution)/shard_map/while
  242.7 0.7 copy-start.3
  242.9 0.6 copy-start.5
  251.5 23.4 %copy-start = (f32[640,640]{1,0:T(8,128)}, f32[640,640]{1,0:T(8,128)S(1)}, u32[]{:S(2)}) copy-start(f32[640,640]{1,0:T(8,128)S(1)} %fusion.201) | copy-start | bytes 4915204 | tf_op jit(solution)/shard_map/while
  273.7 0.8 copy-start.1
  426.1 2.4 copy-start.2
  426.5 6.6 %copy-start.4 = (f32[2,64,128]{2,0,1:T(2,128)S(1)}, f32[2,64,128]{2,0,1:T(2,128)}, u32[]{:S(2)}) copy-start(f32[2,64,128]{2,0,1:T(2,128)} %get-tuple-element.299) | copy-start | bytes 196612 | tf_op jit(solution)/shard_map/while
  433.1 0.7 copy-start.3
  433.3 0.6 copy-start.5
  442.2 24.4 %copy-start.6 = (f32[2,64,128]{2,0,1:T(2,128)S(1)}, f32[2,64,128]{2,0,1:T(2,128)}, u32[]{:S(2)}) copy-start(f32[2,64,128]{2,0,1:T(2,128)} %get-tuple-element.92) | copy-start | bytes 196612
  442.3 8.9 %collective-permute-start.4 = (f32[4,3,32,128]{3,2,1,0:T(8,128)S(1)}, f32[4,3,32,128]{3,2,1,0:T(8,128)S(1)}, u32[]{:S(2)}, u32[]{:S(2)}) collective-permute-start(f32[4,3,32,128]{3,2,1,0:T(8,128)S(1)} %bitcast.219), channel_id=1, source_target_pairs={{4,0},{8,4},{12,8},{5,1},{9,5},{13,9},{6,2},{10,6},{14,10},{7,3},{... | collective-permute-start | bytes 589832 | tf_op jit(solution)/shard_map/ppermute | solution.py:30
  443.7 17.1 %collective-permute-start.5 = (f32[4,3,32,128]{3,2,1,0:T(8,128)S(1)}, f32[4,3,32,128]{3,2,1,0:T(8,128)S(1)}, u32[]{:S(2)}, u32[]{:S(2)}) collective-permute-start(f32[4,3,32,128]{3,2,1,0:T(8,128)S(1)} %bitcast.220), channel_id=1, source_target_pairs={{8,0},{12,4},{9,1},{13,5},{10,2},{14,6},{11,3},{15,7},{24,16},{28,... | collective-permute-start | bytes 589832 | tf_op jit(solution)/shard_map/ppermute | solution.py:30
  460.8 10.3 %collective-permute-start.6 = (f32[4,1,32,128]{3,2,1,0:T(8,128)S(1)}, f32[4,1,32,128]{3,2,1,0:T(8,128)S(1)}, u32[]{:S(2)}, u32[]{:S(2)}) collective-permute-start(f32[4,1,32,128]{3,2,1,0:T(8,128)S(1)} %get-tuple-element.148), channel_id=1, source_target_pairs={{2,0},{3,1},{6,4},{7,5},{10,8},{11,9},{14,12},{15,13},{18,16},{19,... | collective-permute-start | bytes 196616 | tf_op jit(solution)/shard_map/ppermute | solution.py:30
  462.1 9.0 %collective-permute-start.7 = (f32[4,1,32,128]{3,2,1,0:T(8,128)S(1)}, f32[4,1,32,128]{3,2,1,0:T(8,128)S(1)}, u32[]{:S(2)}, u32[]{:S(2)}) collective-permute-start(f32[4,1,32,128]{3,2,1,0:T(8,128)S(1)} %get-tuple-element.149), channel_id=1, source_target_pairs={{0,2},{1,3},{4,6},{5,7},{8,10},{9,11},{12,14},{13,15},{16,18},{17,... | collective-permute-start | bytes 196616 | tf_op jit(solution)/shard_map/ppermute | solution.py:30
Sparse Core Ops, SparseCore 0:
  35.7 14.5 all-gather.1
where the time goes:
time: 481 us; the launch traced here: 479 us
  other arithmetic  313 us (65%)
  local copies, waits for them, and re-layouts  42.5 us (9%)
  waiting for transfers between devices  40.6 us (8%)
  starting transfers between devices  22.6 us (5%)
  matrix products  22.4 us (5%)
  loops' own time  14.5 us (3%)
  between operations  14.5 us (3%)
  blocking collectives  8.84 us (2%)
    another operation x36, other arithmetic, one_block(): factor = jnp.linalg.cholesky(cov)  203 us
    another operation x6, other arithmetic, one_block(): solved = jax.scipy.linalg.solve_triangular(factor, values, lower=True)  98.5 us
    ppermute x6, waiting for transfers between devices, shifted(): return lax.ppermute(block, axis, route)  21.3 us
    another operation x30, local copies, waits for them, and re-layouts  20.1 us
    ppermute x6, starting transfers between devices, shifted(): return lax.ppermute(block, axis, route)  16.4 us
    all_gather x1, waiting for transfers between devices, per_device(): all_fields = lax.all_gather(flat_window[:, 2:], 'fld', axis=1, tiled=True)  14.3 us
    another operation x1, loops' own time, per_device(): lax.map(visit_mine, jnp.arange(half, dtype=jnp.int32))  13.7 us
    another operation x16, matrix products, one_block(): factor = jnp.linalg.cholesky(cov)  12.9 us
  transfers between devices with their start and end apart: 9, of which 7 were waited for; matrix products, arithmetic and copies ran while one was open for 0% of the time, Pallas kernels for 0%

commit v1 on v0

v1 whole, which is shorter than its diff:
```python
import functools

import jax
import jax.numpy as jnp
from jax import lax
from jax.experimental import pallas as pl
from jax.experimental.pallas import tpu as pltpu
from jax.sharding import PartitionSpec as P

ELL = 0.3
NUGGET = 0.25
ROWS = 8
HIGHEST = lax.Precision.HIGHEST


def shifted(block, axis, distance):
    devices = range(lax.axis_size(axis))
    route = [(i - distance, i) for i in devices if i - distance in devices]
    return lax.ppermute(block, axis, route)


def dot(a, b, dims):
    return lax.dot_general(
        a, b, (dims, ((), ())), precision=HIGHEST, preferred_element_type=jnp.float32
    )


def mul(a, b):
    return dot(a, b, ((1,), (0,)))


def mul_tn(a, b):
    return dot(a, b, ((0,), (0,)))


def mul_nt(a, b):
    return dot(a, b, ((1,), (1,)))


def across_lanes(x, lane):
    return jnp.broadcast_to(x[:, lane : lane + 1], x.shape[:1] + (128,))


def across_rows(x, row):
    return jnp.broadcast_to(x[row : row + 1, :], x.shape)


def inverse_factors(mats):
    n = mats[0].shape[0]
    panels = n // ROWS
    row = lax.broadcasted_iota(jnp.int32, (ROWS, n), 0)
    lane = lax.broadcasted_iota(jnp.int32, (ROWS, n), 1)
    count = len(mats)
    s = [[m[ROWS * i : ROWS * (i + 1)] for i in range(panels)] for m in mats]
    q = [
        [jnp.where(lane == row + ROWS * i, 1.0, 0.0).astype(jnp.float32) for i in range(panels)]
        for _ in mats
    ]
    for p in range(panels):
        top = [s[c][p] for c in range(count)]
        inv = [q[c][p] for c in range(count)]
        cols = [[across_lanes(top[c], ROWS * p + j) for j in range(ROWS)] for c in range(count)]
        scale = [jnp.zeros((ROWS, n), jnp.float32) for _ in mats]
        for k in range(ROWS):
            for c in range(count):
                pivot = across_rows(cols[c][k], k)
                scale[c] = jnp.where(row == k, pivot, scale[c])
                if k == ROWS - 1:
                    continue
                m = jnp.where(row > k, cols[c][k] * (1.0 / pivot), 0.0)
                for j in range(k + 1, ROWS):
                    cols[c][j] = cols[c][j] - m * across_rows(cols[c][j], k)
                top[c] = top[c] - m * across_rows(top[c], k)
                inv[c] = inv[c] - m * across_rows(inv[c], k)
        for c in range(count):
            root = lax.rsqrt(scale[c])
            r = top[c] * root
            w = inv[c] * root
            q[c][p] = w
            if p + 1 == panels:
                continue
            rt = r.T
            rk = [across_rows(r, k) for k in range(ROWS)]
            wk = [across_rows(w, k) for k in range(ROWS)]
            for i in range(p + 1, panels):
                part = rt[ROWS * i : ROWS * (i + 1)]
                for k in range(ROWS):
                    coef = across_lanes(part, k)
                    s[c][i] = s[c][i] - coef * rk[k]
                    q[c][i] = q[c][i] - coef * wk[k]
    return [jnp.concatenate(q[c], axis=0) for c in range(count)]


def factor_kernel(slots_ref, masks_ref, window_ref, g_ref, s_ref, w_ref, xc_ref):
    half, width = g_ref.shape[0], g_ref.shape[1]
    n = g_ref.shape[2]
    both = range(half)
    for c in both:
        for t in range(width):
            pts = window_ref[slots_ref[c, t]]
            for d in range(2):
                xc_ref[c, t, d] = jnp.broadcast_to(pts[d : d + 1], (n, n)).T
    eye = lax.broadcasted_iota(jnp.int32, (n, n), 0) == lax.broadcasted_iota(
        jnp.int32, (n, n), 1
    )
    factor = 3.0 / (ELL * ELL)
    for c in both:
        for u in range(width):
            pts = window_ref[slots_ref[c, u]]
            for t in range(u + 1):
                dx = xc_ref[c, t, 0] - pts[0:1]
                dy = xc_ref[c, t, 1] - pts[1:2]
                r2 = (dx * dx + dy * dy) * factor
                scaled = r2 * lax.rsqrt(jnp.maximum(r2, 1e-30))
                value = (1.0 + scaled) * jnp.exp(-scaled)
                value = value * (masks_ref[c, t] * masks_ref[c, u])
                if t == u:
                    m = masks_ref[c, t]
                    value = value + jnp.where(eye, NUGGET * m + 1.0 - m, 0.0)
                s_ref[c, t, u] = value

    def step(t, carry):
        w = inverse_factors([s_ref[c, t, t] for c in both])
        for c in both:
            w_ref[c, t] = w[c]
        for tv in range(width - 1):

            @pl.when(t == tv)
            def _():
                b = [[None] * width for _ in both]
                for u in range(tv + 1, width):
                    for c in both:
                        b[c][u] = mul(w_ref[c, tv], s_ref[c, tv, u])
                        s_ref[c, tv, u] = b[c][u]
                for u in range(tv + 1, width):
                    for x in range(u, width):
                        for c in both:
                            s_ref[c, u, x] = s_ref[c, u, x] - mul_tn(b[c][u], b[c][x])

        return carry

    lax.fori_loop(0, width, step, 0)
    for c in both:
        g_ref[c, width - 1] = w_ref[c, width - 1]
    for t in reversed(range(width - 1)):
        for c in both:
            total = mul_nt(g_ref[c, width - 1], s_ref[c, t, width - 1])
            for u in range(t + 1, width - 1):
                total = total + mul_nt(g_ref[c, u], s_ref[c, t, u])
            g_ref[c, t] = -mul(total, w_ref[c, t])


def apply_kernel(slots_ref, first_ref, mine_ref, other_ref, fields_ref, white_ref, terms_ref):
    half, width = mine_ref.shape[0], mine_ref.shape[1]
    terms_ref[...] = jnp.zeros_like(terms_ref)
    for source, start in ((mine_ref, first_ref[0]), (other_ref, half - first_ref[0])):
        for i in range(half):
            block = start + i
            total = None
            for t in range(width):
                part = mul_nt(fields_ref[slots_ref[block, t]], source[i, t])
                total = part if total is None else total + part
            white_ref[block] = total
            for t in range(width):
                cell = slots_ref[block, t]
                terms_ref[cell] = terms_ref[cell] + mul(total, source[i, t])


def padded(cells):
    return [shifted(cells, "grp", 1), cells, shifted(cells, "grp", -1)]


def window_of(cells):
    wide = jnp.stack(padded(cells[:, 0]), axis=1)
    return jnp.concatenate(
        [shifted(wide, "blk", 2), shifted(wide, "blk", 1), wide], axis=0
    ).reshape((9 * cells.shape[0],) + cells.shape[2:])


def per_device(coords, fields, neighbours):
    per = coords.shape[0]
    local_fields = fields.shape[2]
    n = coords.shape[3]
    groups = lax.axis_size("grp")
    blk_pos = lax.axis_index("blk")
    grp_pos = lax.axis_index("grp")
    coords_window = window_of(coords)
    lists = neighbours.reshape(per, neighbours.shape[2])
    earlier = lists // groups - (blk_pos - 2) * per
    beside = lists % groups - grp_pos + 1
    own_slot = ((2 * per + jnp.arange(per, dtype=jnp.int32)) * 3 + 1)[:, None]
    slots = jnp.concatenate([jnp.where(lists >= 0, earlier * 3 + beside, own_slot), own_slot], axis=1)
    masks = jnp.concatenate(
        [(lists >= 0).astype(jnp.float32), jnp.ones((per, 1), jnp.float32)], axis=1
    )
    width = slots.shape[1]
    half = per // lax.axis_size("fld")
    first = lax.axis_index("fld") * half
    my_slots = lax.dynamic_slice_in_dim(slots, first, half, 0)
    my_masks = lax.dynamic_slice_in_dim(masks, first, half, 0)
    smem = pl.BlockSpec(memory_space=pltpu.SMEM)
    vmem = pl.BlockSpec(memory_space=pltpu.VMEM)
    mine = pl.pallas_call(
        factor_kernel,
        out_shape=jax.ShapeDtypeStruct((half, width, n, n), jnp.float32),
        in_specs=[smem, smem, vmem],
        out_specs=vmem,
        scratch_shapes=[
            pltpu.VMEM((half, width, width, n, n), jnp.float32),
            pltpu.VMEM((half, width, n, n), jnp.float32),
            pltpu.VMEM((half, width, 2, n, n), jnp.float32),
        ],
        cost_estimate=pl.CostEstimate(
            flops=60_000_000_000, bytes_accessed=1_000_000, transcendentals=1_000_000
        ),
        compiler_params=pltpu.CompilerParams(vmem_limit_bytes=32 * 1024 * 1024),
        name="factor",
    )(my_slots, my_masks, coords_window)
    fields_window = window_of(fields)
    other = lax.ppermute(mine, "fld", [(0, 1), (1, 0)])
    whitened, terms = pl.pallas_call(
        apply_kernel,
        out_shape=(
            jax.ShapeDtypeStruct((per, local_fields, n), jnp.float32),
            jax.ShapeDtypeStruct((9 * per, local_fields, n), jnp.float32),
        ),
        in_specs=[smem, smem, vmem, vmem, vmem],
        out_specs=(vmem, vmem),
        compiler_params=pltpu.CompilerParams(vmem_limit_bytes=32 * 1024 * 1024),
        name="apply",
    )(slots, first.reshape(1), mine, other, fields_window)
    terms = terms.reshape(3, per, 3, local_fields, n)
    total = terms[2]
    for distance in (1, 2):
        total = total + shifted(terms[2 - distance], "blk", -distance)
    product = total[:, 1]
    for column, offset in ((0, -1), (2, 1)):
        product = product + shifted(total[:, column], "grp", offset)
    return (whitened[:, None], product[:, None])


def solution(mesh):
    return jax.shard_map(
        per_device,
        mesh=mesh,
        in_specs=(
            P(("parts", "blk"), "grp", None, None),
            P(("parts", "blk"), "grp", "fld", None),
            P(("parts", "blk"), "grp", None),
        ),
        out_specs=(
            P(("parts", "blk"), "grp", "fld", None),
            P(("parts", "blk"), "grp", "fld", None),
        ),
        check_vma=False,
    )
```

time: 481 us -> 131 us (0.27)
  other arithmetic: 313 us -> 0.94 us
  Pallas kernels: 0 us -> 62.1 us
  local copies, waits for them, and re-layouts: 42.5 us -> 0.83 us
  matrix products: 22.4 us -> 0 us
  loops' own time: 14.5 us -> 0 us
  starting transfers between devices: 22.6 us -> 36.6 us
  between operations: 14.5 us -> 0.87 us
  waiting for transfers between devices: 40.6 us -> 28.8 us
  blocking collectives: 8.84 us -> 0 us
    another operation x42 -> x2, other arithmetic: 302 us -> 0.02 us  [window_of(): wide = jnp.stack(padded(cells[:, 0]), axis=1)]
    pallas_call x0 -> x2, Pallas kernels: none -> 62.1 us  [the longest x1 54.6 us: per_device(): pl.pallas_call(factor_kernel, out_shape=jax.ShapeDtypeStruct((half, width...]
    another operation x52 -> x0, matrix products: 21.7 us -> none  [the longest x16 12.9 us: one_block(): factor = jnp.linalg.cholesky(cov)]
    another operation x46 -> x0, local copies, waits for them, and re-layouts: 20.5 us -> none
    ppermute x6 -> x12, starting transfers between devices: 16.4 us -> 36.5 us  [shifted(): return lax.ppermute(block, axis, route)]
    another operation x3 -> x0, loops' own time: 14.5 us -> none  [the longest x1 13.7 us: per_device(): lax.map(visit_mine, jnp.arange(half, dtype=jnp.int32))]
    all_gather x1 -> x0, waiting for transfers between devices: 14.3 us -> none  [per_device(): all_fields = lax.all_gather(flat_window[:, 2:], 'fld', axis=1, tiled=True)]
    dynamic_update_slice x6 -> x0, local copies, waits for them, and re-layouts: 9.97 us -> none  [per_device(): lax.map(visit_mine, jnp.arange(half, dtype=jnp.int32))]
  transfers between devices with their start and end apart: 9 -> 13, of which waited for: 7 -> 9; matrix products, arithmetic and copies ran while one was open for 0% -> 0% of each run, Pallas kernels for 0% -> 0%
where the time goes in v1:
time: 131 us; the launch traced here: 130 us
  Pallas kernels  62.1 us (47%)
  starting transfers between devices  36.6 us (28%)
  waiting for transfers between devices  28.8 us (22%)
    pallas_call x1, Pallas kernels, per_device(): pl.pallas_call(factor_kernel, out_shape=jax.ShapeDtypeStruct((half, width...  54.6 us
    ppermute x12, starting transfers between devices, shifted(): return lax.ppermute(block, axis, route)  36.5 us
    ppermute x12, waiting for transfers between devices, shifted(): return lax.ppermute(block, axis, route)  28.8 us
    pallas_call x1, Pallas kernels, per_device(): pl.pallas_call(apply_kernel, out_shape=(jax.ShapeDtypeStruct((per, local_...  7.58 us
  transfers between devices with their start and end apart: 13, of which 9 were waited for; matrix products, arithmetic and copies ran while one was open for 0% of the time, Pallas kernels for 0%

profile of v1, /device:TPU:0, one launch (start us, length us, event | category | flops | bytes accessed | tf_op | source)
XLA Modules:
  0.0 130.2 jit_solution(853194753746153359)
XLA Ops:
  0.6 1.3 collective-permute-start.1
  1.9 4.8 %collective-permute-start = (f32[4,2,128]{2,1,0:T(2,128)}, f32[4,2,128]{2,1,0:T(2,128)S(1)}, u32[]{:S(2)}, u32[]{:S(2)}) collective-permute-start(f32[4,2,128]{2,1,0:T(2,128)} %bitcast.46), channel_id=1, source_target_pairs={{0,2},{1,3},{4,6},{5,7},{8,10},{9,11},{12,14},{13,15},{16,18},{17,... | collective-permute-start | bytes 12296 | tf_op jit(solution)/shard_map/ppermute | solution.py:19
  6.8 0.0 copy-start.2
  6.8 0.7 copy-done.2
  7.5 0.1 fusion.7
  7.6 0.1 pad_add_fusion.slots_ref
  7.7 0.0 copy-start.1
  7.7 0.0 collective-permute-done.1
  7.7 0.6 collective-permute-done
  8.3 0.1 copy-done.1
  8.4 4.6 %collective-permute-start.3 = (f32[4,3,2,128]{3,2,1,0:T(2,128)S(1)}, f32[4,3,2,128]{3,2,1,0:T(2,128)S(1)}, u32[]{:S(2)}, u32[]{:S(2)}) collective-permute-start(f32[4,3,2,128]{3,2,1,0:T(2,128)S(1)} %pad_maximum_fusion.1), channel_id=1, source_target_pairs={{0,4},{4,8},{8,12},{1,5},{5,9},{9,13},{2,6},{6,10},{10,14},{3,7},{... | collective-permute-start | bytes 36872 | tf_op jit(solution)/shard_map/ppermute | solution.py:19
  13.0 4.5 %collective-permute-start.2 = (f32[4,3,2,128]{3,2,1,0:T(2,128)S(1)}, f32[4,3,2,128]{3,2,1,0:T(2,128)S(1)}, u32[]{:S(2)}, u32[]{:S(2)}) collective-permute-start(f32[4,3,2,128]{3,2,1,0:T(2,128)S(1)} %pad_maximum_fusion.1), channel_id=1, source_target_pairs={{0,8},{4,12},{1,9},{5,13},{2,10},{6,14},{3,11},{7,15},{16,24},{20,... | collective-permute-start | bytes 36872 | tf_op jit(solution)/shard_map/ppermute | solution.py:19
  17.5 0.0 collective-permute-done.3
  17.5 1.4 %collective-permute-done.2 = f32[4,3,2,128]{3,2,1,0:T(2,128)S(1)} collective-permute-done((f32[4,3,2,128]{3,2,1,0:T(2,128)S(1)}, f32[4,3,2,128]{3,2,1,0:T(2,128)S(1)}, u32[]{:S(2)}, u32[]{:S(2)}) %collective-permute-start.2) | collective-permute-done | bytes 12320 | tf_op jit(solution)/shard_map/ppermute | solution.py:19
  18.9 0.0 copy-start
  18.9 54.6 %factor.1.mine_ref = f32[2,5,128,128]{3,2,1,0:T(8,128)S(1)} custom-call(s32[2,5]{1,0:T(2,128)S(1)} %constant_dynamic-slice_fusion.1.slots_ref, f32[2,5]{1,0:T(2,128)S(1)} %constant_dynamic-slice_fusion.masks_ref, f32[36,2,128]{2,1,0:T(2,128)S(1)} %bitcast.35), custom_call_target="tpu_custom_call" | custom-call | flops 60000002048 | bytes 1000000 | tf_op jit(solution)/shard_map/factor/pallas_call | solution.py:203
  73.5 0.1 collective-permute-start.4
  73.6 0.0 copy-done
  73.6 1.3 collective-permute-start.6
  74.9 4.5 %collective-permute-start.5 = (f32[4,32,128]{2,1,0:T(8,128)S(1)}, f32[4,32,128]{2,1,0:T(8,128)S(1)}, u32[]{:S(2)}, u32[]{:S(2)}) collective-permute-start(f32[4,32,128]{2,1,0:T(8,128)S(1)} %bitcast.40), channel_id=1, source_target_pairs={{0,2},{1,3},{4,6},{5,7},{8,10},{9,11},{12,14},{13,15},{16,18},{17,... | collective-permute-start | bytes 196616 | tf_op jit(solution)/shard_map/ppermute | solution.py:19
  79.4 0.5 collective-permute-done.6
  79.9 1.4 %collective-permute-done.5 = f32[4,32,128]{2,1,0:T(8,128)S(1)} collective-permute-done((f32[4,32,128]{2,1,0:T(8,128)S(1)}, f32[4,32,128]{2,1,0:T(8,128)S(1)}, u32[]{:S(2)}, u32[]{:S(2)}) %collective-permute-start.5) | collective-permute-done | bytes 65568 | tf_op jit(solution)/shard_map/ppermute | solution.py:19
  81.3 1.3 collective-permute-start.8
  82.6 5.7 %collective-permute-start.7 = (f32[4,3,32,128]{3,2,1,0:T(8,128)S(1)}, f32[4,3,32,128]{3,2,1,0:T(8,128)S(1)}, u32[]{:S(2)}, u32[]{:S(2)}) collective-permute-start(f32[4,3,32,128]{3,2,1,0:T(8,128)S(1)} %pad_maximum_fusion), channel_id=1, source_target_pairs={{0,8},{4,12},{1,9},{5,13},{2,10},{6,14},{3,11},{7,15},{16,24},{20,... | collective-permute-start | bytes 589832 | tf_op jit(solution)/shard_map/ppermute | solution.py:19
  88.4 0.0 collective-permute-done.8
  88.4 3.7 %collective-permute-done.7 = f32[4,3,32,128]{3,2,1,0:T(8,128)S(1)} collective-permute-done((f32[4,3,32,128]{3,2,1,0:T(8,128)S(1)}, f32[4,3,32,128]{3,2,1,0:T(8,128)S(1)}, u32[]{:S(2)}, u32[]{:S(2)}) %collective-permute-start.7) | collective-permute-done | bytes 196640 | tf_op jit(solution)/shard_map/ppermute | solution.py:19
  92.1 0.0 collective-permute-done.4.other_ref
  92.1 7.6 %apply.1 = (f32[4,32,128]{2,1,0:T(8,128)}, f32[36,32,128]{2,1,0:T(8,128)S(1)}) custom-call(s32[4,5]{1,0:T(4,128)S(1)} %pad_add_fusion.slots_ref, s32[1]{0:T(128)} %bitcast.1.first_ref, f32[2,5,128,128]{3,2,1,0:T(8,128)S(1)} %factor.1.mine_ref, f32[2,5,128,128]{3,2,1,0:T(8,128)S(1)} %collective-permute-done.4.other_ref, f32[36,32,128]{2,1,0:T(8,128)S(1)} %bitcast.34), custom_call_target="tpu_custom_call" | custom-call | tf_op jit(solution)/shard_map/apply/pallas_call | solution.py:221
  99.8 1.3 collective-permute-start.9
  101.1 1.3 collective-permute-start.10
  102.4 10.9 %collective-permute-done.9 = f32[4,3,32,128]{3,2,0,1:T(8,128)S(1)} collective-permute-done((f32[4,3,32,128]{3,2,0,1:T(8,128)S(1)}, f32[4,3,32,128]{3,2,0,1:T(8,128)S(1)}, u32[]{:S(2)}, u32[]{:S(2)}) %collective-permute-start.9) | collective-permute-done | bytes 196640 | tf_op jit(solution)/shard_map/ppermute | solution.py:19
  113.3 8.5 %collective-permute-done.10 = f32[4,3,32,128]{3,2,0,1:T(8,128)S(1)} collective-permute-done((f32[4,3,32,128]{3,2,0,1:T(8,128)S(1)}, f32[4,3,32,128]{3,2,0,1:T(8,128)S(1)}, u32[]{:S(2)}, u32[]{:S(2)}) %collective-permute-start.10) | collective-permute-done | bytes 196640 | tf_op jit(solution)/shard_map/ppermute | solution.py:19
  121.8 1.3 collective-permute-start.11
  123.1 4.5 %collective-permute-start.12 = (f32[4,32,128]{2,1,0:T(8,128)S(1)}, f32[4,32,128]{2,1,0:T(8,128)S(1)}, u32[]{:S(2)}, u32[]{:S(2)}) collective-permute-start(f32[4,32,128]{2,1,0:T(8,128)S(1)} %get-tuple-element.12), channel_id=1, source_target_pairs={{0,2},{1,3},{4,6},{5,7},{8,10},{9,11},{12,14},{13,15},{16,18},{17,... | collective-permute-start | bytes 196616 | tf_op jit(solution)/shard_map/ppermute | solution.py:19
  127.7 0.3 collective-permute-done.11
  128.0 1.6 %collective-permute-done.12 = f32[4,32,128]{2,1,0:T(8,128)S(1)} collective-permute-done((f32[4,32,128]{2,1,0:T(8,128)S(1)}, f32[4,32,128]{2,1,0:T(8,128)S(1)}, u32[]{:S(2)}, u32[]{:S(2)}) %collective-permute-start.12) | collective-permute-done | bytes 65568 | tf_op jit(solution)/shard_map/ppermute | solution.py:19
  129.6 0.6 fusion.3
  (15 shorter events, 0.2 us)
Async XLA Ops:
  0.6 7.0 %collective-permute-start.1 = (f32[4,2,128]{2,1,0:T(2,128)}, f32[4,2,128]{2,1,0:T(2,128)S(1)}, u32[]{:S(2)}, u32[]{:S(2)}) collective-permute-start(f32[4,2,128]{2,1,0:T(2,128)} %bitcast.45), channel_id=1, source_target_pairs={{2,0},{3,1},{6,4},{7,5},{10,8},{11,9},{14,12},{15,13},{18,16},{19,... | collective-permute-start | bytes 12296 | tf_op jit(solution)/shard_map/ppermute | solution.py:19
  1.9 6.4 %collective-permute-start = (f32[4,2,128]{2,1,0:T(2,128)}, f32[4,2,128]{2,1,0:T(2,128)S(1)}, u32[]{:S(2)}, u32[]{:S(2)}) collective-permute-start(f32[4,2,128]{2,1,0:T(2,128)} %bitcast.46), channel_id=1, source_target_pairs={{0,2},{1,3},{4,6},{5,7},{8,10},{9,11},{12,14},{13,15},{16,18},{17,... | collective-permute-start | bytes 12296 | tf_op jit(solution)/shard_map/ppermute | solution.py:19
  6.8 0.7 copy-start.2
  7.7 0.7 copy-start.1
  8.4 9.2 %collective-permute-start.3 = (f32[4,3,2,128]{3,2,1,0:T(2,128)S(1)}, f32[4,3,2,128]{3,2,1,0:T(2,128)S(1)}, u32[]{:S(2)}, u32[]{:S(2)}) collective-permute-start(f32[4,3,2,128]{3,2,1,0:T(2,128)S(1)} %pad_maximum_fusion.1), channel_id=1, source_target_pairs={{0,4},{4,8},{8,12},{1,5},{5,9},{9,13},{2,6},{6,10},{10,14},{3,7},{... | collective-permute-start | bytes 36872 | tf_op jit(solution)/shard_map/ppermute | solution.py:19
  13.0 5.9 %collective-permute-start.2 = (f32[4,3,2,128]{3,2,1,0:T(2,128)S(1)}, f32[4,3,2,128]{3,2,1,0:T(2,128)S(1)}, u32[]{:S(2)}, u32[]{:S(2)}) collective-permute-start(f32[4,3,2,128]{3,2,1,0:T(2,128)S(1)} %pad_maximum_fusion.1), channel_id=1, source_target_pairs={{0,8},{4,12},{1,9},{5,13},{2,10},{6,14},{3,11},{7,15},{16,24},{20,... | collective-permute-start | bytes 36872 | tf_op jit(solution)/shard_map/ppermute | solution.py:19
  18.9 54.7 %copy-start = (f32[4,1,32,128]{3,2,1,0:T(8,128)S(1)}, f32[4,1,32,128]{3,2,1,0:T(8,128)}, u32[]{:S(2)}) copy-start(f32[4,1,32,128]{3,2,1,0:T(8,128)} %param.4) | copy-start | bytes 196612
  73.5 18.6 %collective-permute-start.4 = (f32[2,5,128,128]{3,2,1,0:T(8,128)S(1)}, f32[2,5,128,128]{3,2,1,0:T(8,128)S(1)}, u32[]{:S(2)}, u32[]{:S(2)}) collective-permute-start(f32[2,5,128,128]{3,2,1,0:T(8,128)S(1)} %factor.1.mine_ref), channel_id=1, source_target_pairs={{0,1},{1,0},{2,3},{3,2},{4,5},{5,4},{6,7},{7,6},{8,9},{9,8},{10,11... | collective-permute-start | bytes 1966088 | tf_op jit(solution)/shard_map/ppermute | solution.py:220
  73.6 6.4 %collective-permute-start.6 = (f32[4,32,128]{2,1,0:T(8,128)S(1)}, f32[4,32,128]{2,1,0:T(8,128)S(1)}, u32[]{:S(2)}, u32[]{:S(2)}) collective-permute-start(f32[4,32,128]{2,1,0:T(8,128)S(1)} %bitcast.39), channel_id=1, source_target_pairs={{2,0},{3,1},{6,4},{7,5},{10,8},{11,9},{14,12},{15,13},{18,16},{19,... | collective-permute-start | bytes 196616 | tf_op jit(solution)/shard_map/ppermute | solution.py:19
  74.9 6.4 %collective-permute-start.5 = (f32[4,32,128]{2,1,0:T(8,128)S(1)}, f32[4,32,128]{2,1,0:T(8,128)S(1)}, u32[]{:S(2)}, u32[]{:S(2)}) collective-permute-start(f32[4,32,128]{2,1,0:T(8,128)S(1)} %bitcast.40), channel_id=1, source_target_pairs={{0,2},{1,3},{4,6},{5,7},{8,10},{9,11},{12,14},{13,15},{16,18},{17,... | collective-permute-start | bytes 196616 | tf_op jit(solution)/shard_map/ppermute | solution.py:19
  81.3 7.0 %collective-permute-start.8 = (f32[4,3,32,128]{3,2,1,0:T(8,128)S(1)}, f32[4,3,32,128]{3,2,1,0:T(8,128)S(1)}, u32[]{:S(2)}, u32[]{:S(2)}) collective-permute-start(f32[4,3,32,128]{3,2,1,0:T(8,128)S(1)} %pad_maximum_fusion), channel_id=1, source_target_pairs={{0,4},{4,8},{8,12},{1,5},{5,9},{9,13},{2,6},{6,10},{10,14},{3,7},{... | collective-permute-start | bytes 589832 | tf_op jit(solution)/shard_map/ppermute | solution.py:19
  82.6 9.4 %collective-permute-start.7 = (f32[4,3,32,128]{3,2,1,0:T(8,128)S(1)}, f32[4,3,32,128]{3,2,1,0:T(8,128)S(1)}, u32[]{:S(2)}, u32[]{:S(2)}) collective-permute-start(f32[4,3,32,128]{3,2,1,0:T(8,128)S(1)} %pad_maximum_fusion), channel_id=1, source_target_pairs={{0,8},{4,12},{1,9},{5,13},{2,10},{6,14},{3,11},{7,15},{16,24},{20,... | collective-permute-start | bytes 589832 | tf_op jit(solution)/shard_map/ppermute | solution.py:19
  99.8 13.5 %collective-permute-start.9 = (f32[4,3,32,128]{3,2,0,1:T(8,128)S(1)}, f32[4,3,32,128]{3,2,0,1:T(8,128)S(1)}, u32[]{:S(2)}, u32[]{:S(2)}) collective-permute-start(f32[4,3,32,128]{3,2,0,1:T(8,128)S(1)} %copy.7), channel_id=1, source_target_pairs={{4,0},{8,4},{12,8},{5,1},{9,5},{13,9},{6,2},{10,6},{14,10},{7,3},{... | collective-permute-start | bytes 589832 | tf_op jit(solution)/shard_map/ppermute | solution.py:19
  101.1 20.7 %collective-permute-start.10 = (f32[4,3,32,128]{3,2,0,1:T(8,128)S(1)}, f32[4,3,32,128]{3,2,0,1:T(8,128)S(1)}, u32[]{:S(2)}, u32[]{:S(2)}) collective-permute-start(f32[4,3,32,128]{3,2,0,1:T(8,128)S(1)} %copy.9), channel_id=1, source_target_pairs={{8,0},{12,4},{9,1},{13,5},{10,2},{14,6},{11,3},{15,7},{24,16},{28,... | collective-permute-start | bytes 589832 | tf_op jit(solution)/shard_map/ppermute | solution.py:19
  121.8 6.2 %collective-permute-start.11 = (f32[4,32,128]{2,1,0:T(8,128)S(1)}, f32[4,32,128]{2,1,0:T(8,128)S(1)}, u32[]{:S(2)}, u32[]{:S(2)}) collective-permute-start(f32[4,32,128]{2,1,0:T(8,128)S(1)} %get-tuple-element.11), channel_id=1, source_target_pairs={{2,0},{3,1},{6,4},{7,5},{10,8},{11,9},{14,12},{15,13},{18,16},{19,... | collective-permute-start | bytes 196616 | tf_op jit(solution)/shard_map/ppermute | solution.py:19
  123.1 6.4 %collective-permute-start.12 = (f32[4,32,128]{2,1,0:T(8,128)S(1)}, f32[4,32,128]{2,1,0:T(8,128)S(1)}, u32[]{:S(2)}, u32[]{:S(2)}) collective-permute-start(f32[4,32,128]{2,1,0:T(8,128)S(1)} %get-tuple-element.12), channel_id=1, source_target_pairs={{0,2},{1,3},{4,6},{5,7},{8,10},{9,11},{12,14},{13,15},{16,18},{17,... | collective-permute-start | bytes 196616 | tf_op jit(solution)/shard_map/ppermute | solution.py:19

commit v2 on v1

v2 whole, which is shorter than its diff:
```python
import functools

import jax
import jax.numpy as jnp
from jax import lax
from jax.experimental import pallas as pl
from jax.experimental.pallas import tpu as pltpu
from jax.sharding import PartitionSpec as P

ELL = 0.3
NUGGET = 0.25
ROWS = 8
HIGHEST = lax.Precision.HIGHEST


def dot(a, b, dims):
    return lax.dot_general(
        a, b, (dims, ((), ())), precision=HIGHEST, preferred_element_type=jnp.float32
    )


def mul(a, b):
    return dot(a, b, ((1,), (0,)))


def mul_tn(a, b):
    return dot(a, b, ((0,), (0,)))


def mul_nt(a, b):
    return dot(a, b, ((1,), (1,)))


def across_lanes(x, lane):
    return jnp.broadcast_to(x[:, lane : lane + 1], x.shape[:1] + (128,))


def across_rows(x, row):
    return jnp.broadcast_to(x[row : row + 1, :], x.shape)


def inverse_factors(mats):
    n = mats[0].shape[0]
    panels = n // ROWS
    row = lax.broadcasted_iota(jnp.int32, (ROWS, n), 0)
    lane = lax.broadcasted_iota(jnp.int32, (ROWS, n), 1)
    count = len(mats)
    s = [[m[ROWS * i : ROWS * (i + 1)] for i in range(panels)] for m in mats]
    q = [
        [jnp.where(lane == row + ROWS * i, 1.0, 0.0).astype(jnp.float32) for i in range(panels)]
        for _ in mats
    ]
    for p in range(panels):
        top = [s[c][p] for c in range(count)]
        inv = [q[c][p] for c in range(count)]
        cols = [[across_lanes(top[c], ROWS * p + j) for j in range(ROWS)] for c in range(count)]
        scale = [jnp.zeros((ROWS, n), jnp.float32) for _ in mats]
        for k in range(ROWS):
            for c in range(count):
                pivot = across_rows(cols[c][k], k)
                scale[c] = jnp.where(row == k, pivot, scale[c])
                if k == ROWS - 1:
                    continue
                m = jnp.where(row > k, cols[c][k] * (1.0 / pivot), 0.0)
                for j in range(k + 1, ROWS):
                    cols[c][j] = cols[c][j] - m * across_rows(cols[c][j], k)
                top[c] = top[c] - m * across_rows(top[c], k)
                inv[c] = inv[c] - m * across_rows(inv[c], k)
        for c in range(count):
            root = lax.rsqrt(scale[c])
            r = top[c] * root
            w = inv[c] * root
            q[c][p] = w
            if p + 1 == panels:
                continue
            rt = r.T
            rk = [across_rows(r, k) for k in range(ROWS)]
            wk = [across_rows(w, k) for k in range(ROWS)]
            for i in range(p + 1, panels):
                part = rt[ROWS * i : ROWS * (i + 1)]
                for k in range(ROWS):
                    coef = across_lanes(part, k)
                    s[c][i] = s[c][i] - coef * rk[k]
                    q[c][i] = q[c][i] - coef * wk[k]
    return [jnp.concatenate(q[c], axis=0) for c in range(count)]


def window_kernel(
    slots_ref,
    masks_ref,
    coords_ref,
    fields_ref,
    white_ref,
    product_ref,
    coords_win,
    fields_win,
    s_ref,
    w_ref,
    xc_ref,
    mine_ref,
    other_ref,
    v_ref,
    terms_ref,
    back_ref,
    coords_send,
    coords_recv,
    fields_send,
    fields_recv,
    swap_send,
    swap_recv,
    back_send,
    back_recv,
):
    width, half, n = mine_ref.shape[0], mine_ref.shape[1], mine_ref.shape[2]
    per = fields_ref.shape[0]
    both = range(half)
    blk, grp, fld = (lax.axis_index(a) for a in ("blk", "grp", "fld"))
    blks, grps = lax.axis_size("blk"), lax.axis_size("grp")
    first = fld * half
    partner = {"fld": 1 - fld}
    routes = [(z, x) for z in (2, 1, 0) for x in (-1, 0, 1) if (z, x) != (0, 0)]

    def there(z, x):
        return (blk + z >= 0) & (blk + z < blks) & (grp + x >= 0) & (grp + x < grps)

    def place(z, x):
        return {"blk": blk + z, "grp": grp + x}

    coords_win[...] = jnp.zeros_like(coords_win)
    fields_win[...] = jnp.zeros_like(fields_win)
    barrier = pltpu.get_barrier_semaphore()
    pl.semaphore_signal(barrier, inc=1, device_id=partner, device_id_type=pl.DeviceIdType.MESH)
    around = jnp.int32(1)
    for z in range(-2, 3):
        for x in (-1, 0, 1):
            if (z, x) == (0, 0):
                continue

            @pl.when(there(z, x))
            def _():
                pl.semaphore_signal(
                    barrier, inc=1, device_id=place(z, x), device_id_type=pl.DeviceIdType.MESH
                )

            around = around + there(z, x).astype(jnp.int32)
    pl.semaphore_wait(barrier, around)

    def out_copy(source, window, send, recv, z, x):
        index = routes.index((z, x))
        cell = (2 - z) * 3 + 1 - x
        return pltpu.make_async_remote_copy(
            src_ref=source,
            dst_ref=window.at[pl.ds(cell * per, per)],
            send_sem=send.at[index],
            recv_sem=recv.at[index],
            device_id=place(z, x),
            device_id_type=pl.DeviceIdType.MESH,
        )

    def coords_copy(z, x):
        return out_copy(coords_ref, coords_win, coords_send, coords_recv, z, x)

    def fields_copy(z, x):
        return out_copy(fields_ref, fields_win, fields_send, fields_recv, z, x)

    def back_copy(z, x):
        index = routes.index((z, x))
        cell = (2 - z) * 3 + 1 - x
        return pltpu.make_async_remote_copy(
            src_ref=terms_ref.at[pl.ds(cell * per, per)],
            dst_ref=back_ref.at[index],
            send_sem=back_send.at[index],
            recv_sem=back_recv.at[index],
            device_id=place(-z, -x),
            device_id_type=pl.DeviceIdType.MESH,
        )

    def on(condition, act):
        @pl.when(condition)
        def _():
            act()

    for z, x in routes:
        on(there(z, x), lambda: coords_copy(z, x).start())
    for z, x in routes:
        on(there(z, x), lambda: fields_copy(z, x).start())
    own = (2 * 3 + 1) * per
    coords_win[pl.ds(own, per)] = coords_ref[...]
    fields_win[pl.ds(own, per)] = fields_ref[...]
    for z, x in routes:
        on(there(-z, -x), lambda: coords_copy(z, x).wait_recv())

    def slot(block, t):
        return slots_ref[block, t]

    for c in both:
        for t in range(width):
            pts = coords_win[slot(first + c, t)]
            for d in range(2):
                xc_ref[c, t, d] = jnp.broadcast_to(pts[d : d + 1], (n, n)).T
    eye = lax.broadcasted_iota(jnp.int32, (n, n), 0) == lax.broadcasted_iota(
        jnp.int32, (n, n), 1
    )
    factor = 3.0 / (ELL * ELL)
    for c in both:
        for u in range(width):
            pts = coords_win[slot(first + c, u)]
            mu = masks_ref[first + c, u]
            for t in range(u + 1):
                dx = xc_ref[c, t, 0] - pts[0:1]
                dy = xc_ref[c, t, 1] - pts[1:2]
                r2 = (dx * dx + dy * dy) * factor
                scaled = r2 * lax.rsqrt(jnp.maximum(r2, 1e-30))
                value = (1.0 + scaled) * jnp.exp(-scaled)
                value = value * (masks_ref[first + c, t] * mu)
                if t == u:
                    value = value + jnp.where(eye, NUGGET * mu + 1.0 - mu, 0.0)
                s_ref[c, t, u] = value

    def step(t, carry):
        w = inverse_factors([s_ref[c, t, t] for c in both])
        for c in both:
            w_ref[c, t] = w[c]
        for tv in range(width - 1):

            @pl.when(t == tv)
            def _():
                b = [[None] * width for _ in both]
                for u in range(tv + 1, width):
                    for c in both:
                        b[c][u] = mul(w_ref[c, tv], s_ref[c, tv, u])
                        s_ref[c, tv, u] = b[c][u]
                for u in range(tv + 1, width):
                    for x in range(u, width):
                        for c in both:
                            s_ref[c, u, x] = s_ref[c, u, x] - mul_tn(b[c][u], b[c][x])

        return carry

    lax.fori_loop(0, width, step, 0)

    def swap(t):
        return pltpu.make_async_remote_copy(
            src_ref=mine_ref.at[t],
            dst_ref=other_ref.at[t],
            send_sem=swap_send.at[t],
            recv_sem=swap_recv.at[t],
            device_id=partner,
            device_id_type=pl.DeviceIdType.MESH,
        )

    for t in reversed(range(width)):
        for c in both:
            if t == width - 1:
                mine_ref[t, c] = w_ref[c, t]
                continue
            total = mul_nt(mine_ref[width - 1, c], s_ref[c, t, width - 1])
            for u in range(t + 1, width - 1):
                total = total + mul_nt(mine_ref[u, c], s_ref[c, t, u])
            mine_ref[t, c] = -mul(total, w_ref[c, t])
        swap(t).start()
    for z, x in routes:
        on(there(-z, -x), lambda: fields_copy(z, x).wait_recv())

    def apply(source, start):
        for c in both:
            block = start + c
            total = None
            for t in range(width):
                part = mul_nt(fields_win[slot(block, t)], source[t, c])
                total = part if total is None else total + part
            white_ref[block] = total
            for t in range(width):
                v_ref[block, t] = mul(total, source[t, c])

    apply(mine_ref, first)
    for t in reversed(range(width)):
        swap(t).wait_recv()
    apply(other_ref, half - first)

    def gather_terms(z, x):
        cell = (2 - z) * 3 + 1 - x
        for i in range(per):
            total = None
            if (z, x) == (0, 0):
                total = v_ref[i, width - 1]
            order = (2 - z) * per + i
            for block in range(per):
                if not block <= order < block + 2 * per:
                    continue
                for t in range(width - 1):
                    v = v_ref[block, t]
                    part = jnp.where(slot(block, t) == cell * per + i, v, jnp.zeros_like(v))
                    total = part if total is None else total + part
            if total is None:
                total = jnp.zeros_like(v_ref[0, 0])
            terms_ref[cell * per + i] = total

    for z, x in routes:

        def send_terms(z=z, x=x):
            gather_terms(z, x)
            back_copy(z, x).start()

        on(there(-z, -x), send_terms)
    gather_terms(0, 0)
    product_ref[...] = terms_ref[pl.ds(own, per)]
    for index, (z, x) in enumerate(routes):

        def add_back(z=z, x=x, index=index):
            back_copy(z, x).wait_recv()
            product_ref[...] += back_ref[index]

        on(there(z, x), add_back)
    for t in range(width):
        swap(t).wait_send()
    for z, x in routes:

        def sent(z=z, x=x):
            coords_copy(z, x).wait_send()
            fields_copy(z, x).wait_send()

        on(there(z, x), sent)
        on(there(-z, -x), lambda: back_copy(z, x).wait_send())


def per_device(coords, fields, neighbours):
    per = coords.shape[0]
    local_fields = fields.shape[2]
    n = coords.shape[3]
    groups = lax.axis_size("grp")
    blk_pos = lax.axis_index("blk")
    grp_pos = lax.axis_index("grp")
    lists = neighbours.reshape(per, neighbours.shape[2])
    earlier = lists // groups - (blk_pos - 2) * per
    beside = lists % groups - grp_pos + 1
    listed = ((earlier // per) * 3 + beside) * per + earlier % per
    own_slot = (7 * per + jnp.arange(per, dtype=jnp.int32))[:, None]
    slots = jnp.concatenate([jnp.where(lists >= 0, listed, own_slot), own_slot], axis=1)
    masks = jnp.concatenate(
        [(lists >= 0).astype(jnp.float32), jnp.ones((per, 1), jnp.float32)], axis=1
    )
    width = slots.shape[1]
    half = per // lax.axis_size("fld")
    smem = pl.BlockSpec(memory_space=pltpu.SMEM)
    vmem = pl.BlockSpec(memory_space=pltpu.VMEM)
    block = (per, local_fields, n)
    dma = pltpu.SemaphoreType.DMA
    whitened, product = pl.pallas_call(
        window_kernel,
        out_shape=(jax.ShapeDtypeStruct(block, jnp.float32),) * 2,
        in_specs=[smem, smem, vmem, vmem],
        out_specs=(vmem, vmem),
        scratch_shapes=[
            pltpu.VMEM((9 * per, 2, n), jnp.float32),
            pltpu.VMEM((9 * per, local_fields, n), jnp.float32),
            pltpu.VMEM((half, width, width, n, n), jnp.float32),
            pltpu.VMEM((half, width, n, n), jnp.float32),
            pltpu.VMEM((half, width, 2, n, n), jnp.float32),
            pltpu.VMEM((width, half, n, n), jnp.float32),
            pltpu.VMEM((width, half, n, n), jnp.float32),
            pltpu.VMEM((per, width, local_fields, n), jnp.float32),
            pltpu.VMEM((9 * per, local_fields, n), jnp.float32),
            pltpu.VMEM((8,) + block, jnp.float32),
            dma((8,)),
            dma((8,)),
            dma((8,)),
            dma((8,)),
            dma((width,)),
            dma((width,)),
            dma((8,)),
            dma((8,)),
        ],
        compiler_params=pltpu.CompilerParams(
            vmem_limit_bytes=40 * 1024 * 1024, collective_id=0, has_side_effects=True
        ),
        name="window",
    )(slots, masks, coords.reshape(per, 2, n), fields.reshape(block))
    return (whitened[:, None], product[:, None])


def solution(mesh):
    return jax.shard_map(
        per_device,
        mesh=mesh,
        in_specs=(
            P(("parts", "blk"), "grp", None, None),
            P(("parts", "blk"), "grp", "fld", None),
            P(("parts", "blk"), "grp", None),
        ),
        out_specs=(
            P(("parts", "blk"), "grp", "fld", None),
            P(("parts", "blk"), "grp", "fld", None),
        ),
        check_vma=False,
    )
```

time: 131 us -> 84.6 us (0.65)
  starting transfers between devices: 36.6 us -> 0 us
  waiting for transfers between devices: 28.8 us -> 0 us
  Pallas kernels: 62.1 us -> 80.2 us
  local copies, waits for them, and re-layouts: 0.83 us -> 3.38 us
    ppermute x13 -> x0, starting transfers between devices: 36.6 us -> none  [the longest x12 36.5 us: shifted(): return lax.ppermute(block, axis, route)]
    ppermute x13 -> x0, waiting for transfers between devices: 28.8 us -> none  [the longest x12 28.8 us: shifted(): return lax.ppermute(block, axis, route)]
    pallas_call x2 -> x1, Pallas kernels: 62.1 us -> 80.2 us  [per_device(): pl.pallas_call(window_kernel, out_shape=(jax.ShapeDtypeStruct(block, jnp....]
    unnamed x6 -> x8, local copies, waits for them, and re-layouts: 0.74 us -> 3.38 us
  transfers between devices with their start and end apart: 13 -> 0, of which waited for: 9 -> 0; matrix products, arithmetic and copies ran while one was open for 0% -> 0% of each run, Pallas kernels for 0% -> 0%
where the time goes in v2:
time: 84.6 us; the launch traced here: 84.4 us
  Pallas kernels  80.2 us (95%)
  local copies, waits for them, and re-layouts  3.38 us (4%)
    pallas_call x1, Pallas kernels, per_device(): pl.pallas_call(window_kernel, out_shape=(jax.ShapeDtypeStruct(block, jnp....  80.2 us
    unnamed x8, local copies, waits for them, and re-layouts  3.38 us

profile of v2, /device:TPU:0, one launch (start us, length us, event | category | flops | bytes accessed | tf_op | source)
XLA Modules:
  0.0 84.4 jit_solution(14115116236841053826)
XLA Ops:
  0.6 0.0 copy-start.2
  0.6 0.7 copy-done.2
  1.3 0.1 fusion.5
  1.4 0.0 copy-start.1
  1.4 0.1 pad_add_fusion.slots_ref
  1.5 0.6 copy-done.1
  2.1 0.0 copy-start
  2.1 0.8 copy-done
  2.9 80.2 %window.1 = (f32[4,32,128]{2,1,0:T(8,128)S(1)}, f32[4,32,128]{2,1,0:T(8,128)S(1)}) custom-call(s32[4,5]{1,0:T(4,128)S(1)} %pad_add_fusion.slots_ref, f32[4,5]{1,0:T(4,128)S(1)} %pad_convert_fusion.masks_ref, f32[4,2,128]{2,1,0:T(2,128)S(1)} %bitcast.12, f32[4,32,128]{2,1,0:T(8,128)S(1)} %bitcast.9), custom_call_target="tpu_custom_call" | custom-call | tf_op jit(solution)/shard_map/window/pallas_call | solution.py:349
  83.2 0.6 copy.9
  83.8 0.6 copy.10
  (4 shorter events, 0.0 us)
Async XLA Ops:
  0.6 0.7 copy-start.2
  1.4 0.7 copy-start.1
  2.1 0.8 copy-start

commit v3 on v2

--- a/solution.py
+++ b/solution.py
@@ -45,44 +45,81 @@
     row = lax.broadcasted_iota(jnp.int32, (ROWS, n), 0)
     lane = lax.broadcasted_iota(jnp.int32, (ROWS, n), 1)
     count = len(mats)
+    every = range(count)
     s = [[m[ROWS * i : ROWS * (i + 1)] for i in range(panels)] for m in mats]
     q = [
         [jnp.where(lane == row + ROWS * i, 1.0, 0.0).astype(jnp.float32) for i in range(panels)]
         for _ in mats
     ]
-    for p in range(panels):
-        top = [s[c][p] for c in range(count)]
-        inv = [q[c][p] for c in range(count)]
-        cols = [[across_lanes(top[c], ROWS * p + j) for j in range(ROWS)] for c in range(count)]
-        scale = [jnp.zeros((ROWS, n), jnp.float32) for _ in mats]
-        for k in range(ROWS):
-            for c in range(count):
-                pivot = across_rows(cols[c][k], k)
-                scale[c] = jnp.where(row == k, pivot, scale[c])
-                if k == ROWS - 1:
-                    continue
-                m = jnp.where(row > k, cols[c][k] * (1.0 / pivot), 0.0)
-                for j in range(k + 1, ROWS):
-                    cols[c][j] = cols[c][j] - m * across_rows(cols[c][j], k)
-                top[c] = top[c] - m * across_rows(top[c], k)
-                inv[c] = inv[c] - m * across_rows(inv[c], k)
-        for c in range(count):
-            root = lax.rsqrt(scale[c])
-            r = top[c] * root
-            w = inv[c] * root
-            q[c][p] = w
-            if p + 1 == panels:
+    leaf = 2 * ROWS
+    for p in range(0, panels, 2):
+        top = [[s[c][p + h] for h in range(2)] for c in every]
+        inv = [[q[c][p + h] for h in range(2)] for c in every]
+        cols = [
+            [[across_lanes(top[c][h], ROWS * p + j) for j in range(leaf)] for h in range(2)]
+            for c in every
+        ]
+        scale = [[None, None] for _ in mats]
+        for k in range(0, leaf, 2):
+            g, k0 = k // ROWS, k % ROWS
+            k1 = k0 + 1
+            for c in every:
+                x = cols[c]
+                pa = across_rows(x[g][k], k0)
+                pb = across_rows(x[g][k + 1], k0)
+                pc = across_rows(x[g][k + 1], k1)
+                det = pa * pc - pb * pb
+                over = 1.0 / det
+                over_a = 1.0 / pa
+                old = jnp.ones_like(pa) if scale[c][g] is None else scale[c][g]
+                scale[c][g] = jnp.where(row == k0, pa, jnp.where(row == k1, det * over_a, old))
+                rows_j = {
+                    j: (across_rows(x[g][j], k0), across_rows(x[g][j], k1))
+                    for j in range(k + 2, leaf)
+                }
+                top_k = (across_rows(top[c][g], k0), across_rows(top[c][g], k1))
+                inv_k = (across_rows(inv[c][g], k0), across_rows(inv[c][g], k1))
+                for h in range(g, 2):
+                    n0 = pc * x[h][k] - pb * x[h][k + 1]
+                    n1 = pa * x[h][k + 1] - pb * x[h][k]
+                    if h == g:
+                        n0 = jnp.where(row > k1, n0, 0.0)
+                        n1 = jnp.where(row > k1, n1, 0.0)
+                    m0 = n0 * over
+                    m1 = n1 * over
+                    if not (h == g and k1 == ROWS - 1):
+                        for j in range(k + 2, leaf):
+                            u0, u1 = rows_j[j]
+                            if j < k + 4:
+                                x[h][j] = x[h][j] - (n0 * u0 + n1 * u1) * over
+                            else:
+                                x[h][j] = x[h][j] - (m0 * u0 + m1 * u1)
+                    if h == g:
+                        m0 = jnp.where(row == k1, pb * over_a, m0)
+                    top[c][h] = top[c][h] - (m0 * top_k[0] + m1 * top_k[1])
+                    inv[c][h] = inv[c][h] - (m0 * inv_k[0] + m1 * inv_k[1])
+        for c in every:
+            roots = [lax.rsqrt(scale[c][h]) for h in range(2)]
+            r = [top[c][h] * roots[h] for h in range(2)]
+            w = [inv[c][h] * roots[h] for h in range(2)]
+            for h in range(2):
+                q[c][p + h] = w[h]
+            if p + 2 == panels:
                 continue
-            rt = r.T
-            rk = [across_rows(r, k) for k in range(ROWS)]
-            wk = [across_rows(w, k) for k in range(ROWS)]
-            for i in range(p + 1, panels):
+            rt = jnp.concatenate(r, axis=0).T
+            rk = [across_rows(r[k // ROWS], k % ROWS) for k in range(leaf)]
+            wk = [across_rows(w[k // ROWS], k % ROWS) for k in range(leaf)]
+            for i in range(p + 2, panels):
                 part = rt[ROWS * i : ROWS * (i + 1)]
-                for k in range(ROWS):
-                    coef = across_lanes(part, k)
-                    s[c][i] = s[c][i] - coef * rk[k]
-                    q[c][i] = q[c][i] - coef * wk[k]
-    return [jnp.concatenate(q[c], axis=0) for c in range(count)]
+                sums = [None, None]
+                for k in range(0, leaf, 2):
+                    c0, c1 = across_lanes(part, k), across_lanes(part, k + 1)
+                    for index, held in enumerate((rk, wk)):
+                        both = c0 * held[k] + c1 * held[k + 1]
+                        sums[index] = both if sums[index] is None else sums[index] + both
+                s[c][i] = s[c][i] - sums[0]
+                q[c][i] = q[c][i] - sums[1]
+    return [jnp.concatenate(q[c], axis=0) for c in every]
 
 
 def window_kernel(
@@ -111,7 +148,8 @@
     back_send,
     back_recv,
 ):
-    width, half, n = mine_ref.shape[0], mine_ref.shape[1], mine_ref.shape[2]
+    half, n = mine_ref.shape[0], mine_ref.shape[1]
+    width = mine_ref.shape[2] // n
     per = fields_ref.shape[0]
     both = range(half)
     blk, grp, fld = (lax.axis_index(a) for a in ("blk", "grp", "fld"))
@@ -215,34 +253,35 @@
                 value = value * (masks_ref[first + c, t] * mu)
                 if t == u:
                     value = value + jnp.where(eye, NUGGET * mu + 1.0 - mu, 0.0)
-                s_ref[c, t, u] = value
+                s_ref[c, t, :, u * n : (u + 1) * n] = value
 
     def step(t, carry):
-        w = inverse_factors([s_ref[c, t, t] for c in both])
+        w = inverse_factors([s_ref[c, t, :, pl.ds(pl.multiple_of(t * n, n), n)] for c in both])
         for c in both:
             w_ref[c, t] = w[c]
         for tv in range(width - 1):
 
             @pl.when(t == tv)
             def _():
-                b = [[None] * width for _ in both]
+                b = [mul(w_ref[c, tv], s_ref[c, tv, :, (tv + 1) * n :]) for c in both]
+                for c in both:
+                    s_ref[c, tv, :, (tv + 1) * n :] = b[c]
                 for u in range(tv + 1, width):
+                    skip = (u - tv - 1) * n
                     for c in both:
-                        b[c][u] = mul(w_ref[c, tv], s_ref[c, tv, u])
-                        s_ref[c, tv, u] = b[c][u]
-                for u in range(tv + 1, width):
-                    for x in range(u, width):
-                        for c in both:
-                            s_ref[c, u, x] = s_ref[c, u, x] - mul_tn(b[c][u], b[c][x])
+                        s_ref[c, u, :, u * n :] = s_ref[c, u, :, u * n :] - mul_tn(
+                            b[c][:, skip : skip + n], b[c][:, skip:]
+                        )
 
         return carry
 
     lax.fori_loop(0, width, step, 0)
 
     def swap(t):
+        piece = pl.ds(t * n, n)
         return pltpu.make_async_remote_copy(
-            src_ref=mine_ref.at[t],
-            dst_ref=other_ref.at[t],
+            src_ref=mine_ref.at[:, :, piece],
+            dst_ref=other_ref.at[:, :, piece],
             send_sem=swap_send.at[t],
             recv_sem=swap_recv.at[t],
             device_id=partner,
@@ -252,12 +291,11 @@
     for t in reversed(range(width)):
         for c in both:
             if t == width - 1:
-                mine_ref[t, c] = w_ref[c, t]
+                mine_ref[c, :, t * n :] = w_ref[c, t]
                 continue
-            total = mul_nt(mine_ref[width - 1, c], s_ref[c, t, width - 1])
-            for u in range(t + 1, width - 1):
-                total = total + mul_nt(mine_ref[u, c], s_ref[c, t, u])
-            mine_ref[t, c] = -mul(total, w_ref[c, t])
+            later = (t + 1) * n
+            total = mul_nt(mine_ref[c, :, later:], s_ref[c, t, :, later:])
+            mine_ref[c, :, t * n : later] = -mul(total, w_ref[c, t])
         swap(t).start()
     for z, x in routes:
         on(there(-z, -x), lambda: fields_copy(z, x).wait_recv())
@@ -265,13 +303,10 @@
     def apply(source, start):
         for c in both:
             block = start + c
-            total = None
-            for t in range(width):
-                part = mul_nt(fields_win[slot(block, t)], source[t, c])
-                total = part if total is None else total + part
+            values = jnp.concatenate([fields_win[slot(block, t)] for t in range(width)], axis=1)
+            total = mul_nt(values, source[c])
             white_ref[block] = total
-            for t in range(width):
-                v_ref[block, t] = mul(total, source[t, c])
+            v_ref[block] = mul(total, source[c])
 
     apply(mine_ref, first)
     for t in reversed(range(width)):
@@ -283,17 +318,17 @@
         for i in range(per):
             total = None
             if (z, x) == (0, 0):
-                total = v_ref[i, width - 1]
+                total = v_ref[i, :, (width - 1) * n :]
             order = (2 - z) * per + i
             for block in range(per):
                 if not block <= order < block + 2 * per:
                     continue
                 for t in range(width - 1):
-                    v = v_ref[block, t]
+                    v = v_ref[block, :, t * n : (t + 1) * n]
                     part = jnp.where(slot(block, t) == cell * per + i, v, jnp.zeros_like(v))
                     total = part if total is None else total + part
             if total is None:
-                total = jnp.zeros_like(v_ref[0, 0])
+                total = jnp.zeros_like(terms_ref[0])
             terms_ref[cell * per + i] = total
 
     for z, x in routes:
@@ -354,12 +389,12 @@
         scratch_shapes=[
             pltpu.VMEM((9 * per, 2, n), jnp.float32),
             pltpu.VMEM((9 * per, local_fields, n), jnp.float32),
-            pltpu.VMEM((half, width, width, n, n), jnp.float32),
+            pltpu.VMEM((half, width, n, width * n), jnp.float32),
             pltpu.VMEM((half, width, n, n), jnp.float32),
             pltpu.VMEM((half, width, 2, n, n), jnp.float32),
-            pltpu.VMEM((width, half, n, n), jnp.float32),
-            pltpu.VMEM((width, half, n, n), jnp.float32),
-            pltpu.VMEM((per, width, local_fields, n), jnp.float32),
+            pltpu.VMEM((half, n, width * n), jnp.float32),
+            pltpu.VMEM((half, n, width * n), jnp.float32),
+            pltpu.VMEM((per, local_fields, width * n), jnp.float32),
             pltpu.VMEM((9 * per, local_fields, n), jnp.float32),
             pltpu.VMEM((8,) + block, jnp.float32),
             dma((8,)),

time: 84.6 us -> 76.6 us (0.905)
  Pallas kernels: 80.2 us -> 72.2 us
    pallas_call x1, Pallas kernels: 80.2 us -> 72.2 us  [per_device(): pl.pallas_call(window_kernel, out_shape=(jax.ShapeDtypeStruct(block, jnp....]
where the time goes in v3:
time: 76.6 us; the launch traced here: 76.4 us
  Pallas kernels  72.2 us (94%)
  local copies, waits for them, and re-layouts  3.38 us (4%)
    pallas_call x1, Pallas kernels, per_device(): pl.pallas_call(window_kernel, out_shape=(jax.ShapeDtypeStruct(block, jnp....  72.2 us
    unnamed x8, local copies, waits for them, and re-layouts  3.38 us

profile of v3, /device:TPU:0, one launch (start us, length us, event | category | flops | bytes accessed | tf_op | source)
XLA Modules:
  0.0 76.4 jit_solution(3709322084821064119)
XLA Ops:
  0.6 0.0 copy-start.2
  0.6 0.7 copy-done.2
  1.3 0.1 fusion.5
  1.4 0.0 copy-start.1
  1.4 0.1 pad_add_fusion.slots_ref
  1.5 0.6 copy-done.1
  2.1 0.0 copy-start
  2.1 0.8 %copy-done = f32[4,1,32,128]{3,2,1,0:T(8,128)S(1)} copy-done((f32[4,1,32,128]{3,2,1,0:T(8,128)S(1)}, f32[4,1,32,128]{3,2,1,0:T(8,128)}, u32[]{:S(2)}) %copy-start) | copy-done | bytes 65560
  2.9 72.2 %window.1 = (f32[4,32,128]{2,1,0:T(8,128)S(1)}, f32[4,32,128]{2,1,0:T(8,128)S(1)}) custom-call(s32[4,5]{1,0:T(4,128)S(1)} %pad_add_fusion.slots_ref, f32[4,5]{1,0:T(4,128)S(1)} %pad_convert_fusion.masks_ref, f32[4,2,128]{2,1,0:T(2,128)S(1)} %bitcast.12, f32[4,32,128]{2,1,0:T(8,128)S(1)} %bitcast.9), custom_call_target="tpu_custom_call" | custom-call | tf_op jit(solution)/shard_map/window/pallas_call | solution.py:384
  75.1 0.6 copy.9
  75.8 0.6 copy.10
  (4 shorter events, 0.0 us)
Async XLA Ops:
  0.6 0.7 copy-start.2
  1.4 0.7 copy-start.1
  2.1 0.8 %copy-start = (f32[4,1,32,128]{3,2,1,0:T(8,128)S(1)}, f32[4,1,32,128]{3,2,1,0:T(8,128)}, u32[]{:S(2)}) copy-start(f32[4,1,32,128]{3,2,1,0:T(8,128)} %param.4) | copy-start | bytes 196612

commit v4 on v3

--- a/solution.py
+++ b/solution.py
@@ -39,87 +39,109 @@
     return jnp.broadcast_to(x[row : row + 1, :], x.shape)
 
 
-def inverse_factors(mats):
-    n = mats[0].shape[0]
-    panels = n // ROWS
+def packed_factors(pair):
+    m, n = pair.shape
+    panels = m // ROWS
     row = lax.broadcasted_iota(jnp.int32, (ROWS, n), 0)
     lane = lax.broadcasted_iota(jnp.int32, (ROWS, n), 1)
-    count = len(mats)
-    every = range(count)
-    s = [[m[ROWS * i : ROWS * (i + 1)] for i in range(panels)] for m in mats]
+    left = lane < m
+    s = [pair[ROWS * i : ROWS * (i + 1)] for i in range(panels)]
     q = [
-        [jnp.where(lane == row + ROWS * i, 1.0, 0.0).astype(jnp.float32) for i in range(panels)]
-        for _ in mats
+        jnp.where(lane % m == row + ROWS * i, 1.0, 0.0).astype(jnp.float32) for i in range(panels)
     ]
     leaf = 2 * ROWS
     for p in range(0, panels, 2):
-        top = [[s[c][p + h] for h in range(2)] for c in every]
-        inv = [[q[c][p + h] for h in range(2)] for c in every]
-        cols = [
-            [[across_lanes(top[c][h], ROWS * p + j) for j in range(leaf)] for h in range(2)]
-            for c in every
+        top = [s[p], s[p + 1]]
+        inv = [q[p], q[p + 1]]
+        x = [
+            [
+                jnp.where(
+                    left,
+                    across_lanes(top[h], ROWS * p + j),
+                    across_lanes(top[h], m + ROWS * p + j),
+                )
+                for j in range(leaf)
+            ]
+            for h in range(2)
         ]
-        scale = [[None, None] for _ in mats]
+        scale = [jnp.ones_like(top[0]) for _ in range(2)]
         for k in range(0, leaf, 2):
             g, k0 = k // ROWS, k % ROWS
             k1 = k0 + 1
-            for c in every:
-                x = cols[c]
-                pa = across_rows(x[g][k], k0)
-                pb = across_rows(x[g][k + 1], k0)
-                pc = across_rows(x[g][k + 1], k1)
-                det = pa * pc - pb * pb
-                over = 1.0 / det
-                over_a = 1.0 / pa
-                old = jnp.ones_like(pa) if scale[c][g] is None else scale[c][g]
-                scale[c][g] = jnp.where(row == k0, pa, jnp.where(row == k1, det * over_a, old))
-                rows_j = {
-                    j: (across_rows(x[g][j], k0), across_rows(x[g][j], k1))
-                    for j in range(k + 2, leaf)
-                }
-                top_k = (across_rows(top[c][g], k0), across_rows(top[c][g], k1))
-                inv_k = (across_rows(inv[c][g], k0), across_rows(inv[c][g], k1))
-                for h in range(g, 2):
-                    n0 = pc * x[h][k] - pb * x[h][k + 1]
-                    n1 = pa * x[h][k + 1] - pb * x[h][k]
-                    if h == g:
-                        n0 = jnp.where(row > k1, n0, 0.0)
-                        n1 = jnp.where(row > k1, n1, 0.0)
-                    m0 = n0 * over
-                    m1 = n1 * over
-                    if not (h == g and k1 == ROWS - 1):
-                        for j in range(k + 2, leaf):
-                            u0, u1 = rows_j[j]
-                            if j < k + 4:
-                                x[h][j] = x[h][j] - (n0 * u0 + n1 * u1) * over
-                            else:
-                                x[h][j] = x[h][j] - (m0 * u0 + m1 * u1)
-                    if h == g:
-                        m0 = jnp.where(row == k1, pb * over_a, m0)
-                    top[c][h] = top[c][h] - (m0 * top_k[0] + m1 * top_k[1])
-                    inv[c][h] = inv[c][h] - (m0 * inv_k[0] + m1 * inv_k[1])
-        for c in every:
-            roots = [lax.rsqrt(scale[c][h]) for h in range(2)]
-            r = [top[c][h] * roots[h] for h in range(2)]
-            w = [inv[c][h] * roots[h] for h in range(2)]
-            for h in range(2):
-                q[c][p + h] = w[h]
-            if p + 2 == panels:
-                continue
-            rt = jnp.concatenate(r, axis=0).T
-            rk = [across_rows(r[k // ROWS], k % ROWS) for k in range(leaf)]
-            wk = [across_rows(w[k // ROWS], k % ROWS) for k in range(leaf)]
-            for i in range(p + 2, panels):
-                part = rt[ROWS * i : ROWS * (i + 1)]
-                sums = [None, None]
-                for k in range(0, leaf, 2):
-                    c0, c1 = across_lanes(part, k), across_lanes(part, k + 1)
-                    for index, held in enumerate((rk, wk)):
-                        both = c0 * held[k] + c1 * held[k + 1]
-                        sums[index] = both if sums[index] is None else sums[index] + both
-                s[c][i] = s[c][i] - sums[0]
-                q[c][i] = q[c][i] - sums[1]
-    return [jnp.concatenate(q[c], axis=0) for c in every]
+            pa = across_rows(x[g][k], k0)
+            pb = across_rows(x[g][k + 1], k0)
+            pc = across_rows(x[g][k + 1], k1)
+            det = pa * pc - pb * pb
+            over = 1.0 / det
+            over_a = 1.0 / pa
+            scale[g] = jnp.where(row == k0, pa, jnp.where(row == k1, det * over_a, scale[g]))
+            rows_j = {
+                j: (across_rows(x[g][j], k0), across_rows(x[g][j], k1))
+                for j in range(k + 2, leaf)
+            }
+            top_k = (across_rows(top[g], k0), across_rows(top[g], k1))
+            inv_k = (across_rows(inv[g], k0), across_rows(inv[g], k1))
+            for h in range(g, 2):
+                n0 = pc * x[h][k] - pb * x[h][k + 1]
+                n1 = pa * x[h][k + 1] - pb * x[h][k]
+                if h == g:
+                    n0 = jnp.where(row > k1, n0, 0.0)
+                    n1 = jnp.where(row > k1, n1, 0.0)
+                m0 = n0 * over
+                m1 = n1 * over
+                if not (h == g and k1 == ROWS - 1):
+                    for j in range(k + 2, leaf):
+                        u0, u1 = rows_j[j]
+                        if j < k + 4:
+                            x[h][j] = x[h][j] - (n0 * u0 + n1 * u1) * over
+                        else:
+                            x[h][j] = x[h][j] - (m0 * u0 + m1 * u1)
+                if h == g:
+                    m0 = jnp.where(row == k1, pb * over_a, m0)
+                top[h] = top[h] - (m0 * top_k[0] + m1 * top_k[1])
+                inv[h] = inv[h] - (m0 * inv_k[0] + m1 * inv_k[1])
+        roots = [lax.rsqrt(scale[h]) for h in range(2)]
+        r = [top[h] * roots[h] for h in range(2)]
+        w = [inv[h] * roots[h] for h in range(2)]
+        q[p], q[p + 1] = w
+        if p + 2 == panels:
+            continue
+        rt = jnp.concatenate(r, axis=0).T
+        rk = [across_rows(r[k // ROWS], k % ROWS) for k in range(leaf)]
+        wk = [across_rows(w[k // ROWS], k % ROWS) for k in range(leaf)]
+        for i in range(p + 2, panels):
+            parts = [rt[h * m + ROWS * i : h * m + ROWS * (i + 1)] for h in range(2)]
+            coefs = [
+                jnp.where(left, across_lanes(parts[0], k), across_lanes(parts[1], k))
+                for k in range(leaf)
+            ]
+            sums = [None, None]
+            for k in range(0, leaf, 2):
+                for index, held in enumerate((rk, wk)):
+                    both = coefs[k] * held[k] + coefs[k + 1] * held[k + 1]
+                    sums[index] = both if sums[index] is None else sums[index] + both
+            s[i] = s[i] - sums[0]
+            q[i] = q[i] - sums[1]
+    return jnp.concatenate(q, axis=0)
+
+
+def inverse_factors(mats):
+    m = mats[0].shape[0] // 2
+    w11 = packed_factors(jnp.concatenate([s[:m, :m] for s in mats], axis=1))
+    w11 = [w11[:, :m], w11[:, m:]]
+    r12 = [mul(w, s[:m, m:]) for w, s in zip(w11, mats)]
+    w22 = packed_factors(
+        jnp.concatenate([s[m:, m:] - mul_tn(r, r) for r, s in zip(r12, mats)], axis=1)
+    )
+    w22 = [w22[:, :m], w22[:, m:]]
+    w21 = [-mul(w, mul_tn(r, v)) for w, r, v in zip(w22, r12, w11)]
+    zero = jnp.zeros((m, m), jnp.float32)
+    return [
+        jnp.concatenate(
+            [jnp.concatenate([a, zero], axis=1), jnp.concatenate([b, c], axis=1)], axis=0
+        )
+        for a, b, c in zip(w11, w21, w22)
+    ]
 
 
 def window_kernel(

time: 76.6 us -> 59.7 us (0.78)
  Pallas kernels: 72.2 us -> 55.3 us
    pallas_call x1, Pallas kernels: 72.2 us -> 55.3 us  [per_device(): pl.pallas_call(window_kernel, out_shape=(jax.ShapeDtypeStruct(block, jnp....]
where the time goes in v4:
time: 59.7 us; the launch traced here: 59.5 us
  Pallas kernels  55.3 us (93%)
  local copies, waits for them, and re-layouts  3.38 us (6%)
  between operations  0.66 us (1%)
    pallas_call x1, Pallas kernels, per_device(): pl.pallas_call(window_kernel, out_shape=(jax.ShapeDtypeStruct(block, jnp....  55.3 us
    unnamed x8, local copies, waits for them, and re-layouts  3.38 us

profile of v4, /device:TPU:0, one launch (start us, length us, event | category | flops | bytes accessed | tf_op | source)
XLA Modules:
  0.0 59.5 jit_solution(4861198126474279932)
XLA Ops:
  0.6 0.0 copy-start.2
  0.6 0.7 %copy-done.2 = s32[4,1,4]{2,1,0:T(1,128)S(1)} copy-done((s32[4,1,4]{2,1,0:T(1,128)S(1)}, s32[4,1,4]{2,1,0:T(1,128)}, u32[]{:S(2)}) %copy-start.2) | copy-done | bytes 88
  1.3 0.1 fusion.5
  1.4 0.0 copy-start.1
  1.4 0.1 pad_add_fusion.slots_ref
  1.5 0.6 %copy-done.1 = f32[4,1,2,128]{3,2,1,0:T(2,128)S(1)} copy-done((f32[4,1,2,128]{3,2,1,0:T(2,128)S(1)}, f32[4,1,2,128]{3,2,1,0:T(2,128)}, u32[]{:S(2)}) %copy-start.1) | copy-done | bytes 4120
  2.1 0.0 copy-start
  2.1 0.8 %copy-done = f32[4,1,32,128]{3,2,1,0:T(8,128)S(1)} copy-done((f32[4,1,32,128]{3,2,1,0:T(8,128)S(1)}, f32[4,1,32,128]{3,2,1,0:T(8,128)}, u32[]{:S(2)}) %copy-start) | copy-done | bytes 65560
  2.9 55.3 %window.1 = (f32[4,32,128]{2,1,0:T(8,128)S(1)}, f32[4,32,128]{2,1,0:T(8,128)S(1)}) custom-call(s32[4,5]{1,0:T(4,128)S(1)} %pad_add_fusion.slots_ref, f32[4,5]{1,0:T(4,128)S(1)} %pad_convert_fusion.masks_ref, f32[4,2,128]{2,1,0:T(2,128)S(1)} %bitcast.12, f32[4,32,128]{2,1,0:T(8,128)S(1)} %bitcast.9), custom_call_target="tpu_custom_call" | custom-call | tf_op jit(solution)/shard_map/window/pallas_call | solution.py:406
  58.2 0.6 %copy.9 = f32[4,1,32,128]{3,2,1,0:T(8,128)} copy(f32[4,1,32,128]{3,2,1,0:T(8,128)S(1)} %bitcast.11) | data formatting | bytes 131072
  58.9 0.6 %copy.10 = f32[4,1,32,128]{3,2,1,0:T(8,128)} copy(f32[4,1,32,128]{3,2,1,0:T(8,128)S(1)} %bitcast.10) | data formatting | bytes 131072
  (4 shorter events, 0.0 us)
Async XLA Ops:
  0.6 0.7 %copy-start.2 = (s32[4,1,4]{2,1,0:T(1,128)S(1)}, s32[4,1,4]{2,1,0:T(1,128)}, u32[]{:S(2)}) copy-start(s32[4,1,4]{2,1,0:T(1,128)} %param.5) | copy-start | bytes 196
  1.4 0.7 %copy-start.1 = (f32[4,1,2,128]{3,2,1,0:T(2,128)S(1)}, f32[4,1,2,128]{3,2,1,0:T(2,128)}, u32[]{:S(2)}) copy-start(f32[4,1,2,128]{3,2,1,0:T(2,128)} %param.3) | copy-start | bytes 12292
  2.1 0.8 %copy-start = (f32[4,1,32,128]{3,2,1,0:T(8,128)S(1)}, f32[4,1,32,128]{3,2,1,0:T(8,128)}, u32[]{:S(2)}) copy-start(f32[4,1,32,128]{3,2,1,0:T(8,128)} %param.4) | copy-start | bytes 196612

commit v5 on v4

--- a/solution.py
+++ b/solution.py
@@ -277,27 +277,29 @@
                     value = value + jnp.where(eye, NUGGET * mu + 1.0 - mu, 0.0)
                 s_ref[c, t, :, u * n : (u + 1) * n] = value
 
-    def step(t, carry):
-        w = inverse_factors([s_ref[c, t, :, pl.ds(pl.multiple_of(t * n, n), n)] for c in both])
+    diagonal = [s_ref[c, 0, :, :n] for c in both]
+    for t in range(width):
+        w = inverse_factors(diagonal)
         for c in both:
             w_ref[c, t] = w[c]
-        for tv in range(width - 1):
-
-            @pl.when(t == tv)
-            def _():
-                b = [mul(w_ref[c, tv], s_ref[c, tv, :, (tv + 1) * n :]) for c in both]
-                for c in both:
-                    s_ref[c, tv, :, (tv + 1) * n :] = b[c]
-                for u in range(tv + 1, width):
-                    skip = (u - tv - 1) * n
-                    for c in both:
-                        s_ref[c, u, :, u * n :] = s_ref[c, u, :, u * n :] - mul_tn(
-                            b[c][:, skip : skip + n], b[c][:, skip:]
-                        )
-
-        return carry
-
-    lax.fori_loop(0, width, step, 0)
+        if t + 1 == width:
+            break
+        near = slice((t + 1) * n, (t + 2) * n)
+        far = slice((t + 2) * n, width * n)
+        b = [mul(w[c], s_ref[c, t, :, near]) for c in both]
+        diagonal = [s_ref[c, t + 1, :, near] - mul_tn(b[c], b[c]) for c in both]
+        for c in both:
+            s_ref[c, t, :, near] = b[c]
+            if t + 2 == width:
+                continue
+            rest = mul(w[c], s_ref[c, t, :, far])
+            s_ref[c, t, :, far] = rest
+            s_ref[c, t + 1, :, far] = s_ref[c, t + 1, :, far] - mul_tn(b[c], rest)
+            for u in range(t + 2, width):
+                skip = (u - t - 2) * n
+                s_ref[c, u, :, u * n :] = s_ref[c, u, :, u * n :] - mul_tn(
+                    rest[:, skip : skip + n], rest[:, skip:]
+                )
 
     def swap(t):
         piece = pl.ds(t * n, n)

time: 59.7 us -> 57.4 us (0.961)
  Pallas kernels: 55.3 us -> 53 us
    pallas_call x1, Pallas kernels: 55.3 us -> 53 us  [per_device(): pl.pallas_call(window_kernel, out_shape=(jax.ShapeDtypeStruct(block, jnp....]
where the time goes in v5:
time: 57.4 us; the launch traced here: 57.2 us
  Pallas kernels  53 us (92%)
  local copies, waits for them, and re-layouts  3.38 us (6%)
  between operations  0.66 us (1%)
    pallas_call x1, Pallas kernels, per_device(): pl.pallas_call(window_kernel, out_shape=(jax.ShapeDtypeStruct(block, jnp....  53 us
    unnamed x8, local copies, waits for them, and re-layouts  3.38 us

profile of v5, /device:TPU:0, one launch (start us, length us, event | category | flops | bytes accessed | tf_op | source)
XLA Modules:
  0.0 57.2 jit_solution(2811205258881534443)
XLA Ops:
  0.6 0.0 copy-start.2
  0.6 0.7 %copy-done.2 = s32[4,1,4]{2,1,0:T(1,128)S(1)} copy-done((s32[4,1,4]{2,1,0:T(1,128)S(1)}, s32[4,1,4]{2,1,0:T(1,128)}, u32[]{:S(2)}) %copy-start.2) | copy-done | bytes 88
  1.3 0.1 fusion.5
  1.4 0.0 copy-start.1
  1.4 0.1 pad_add_fusion.slots_ref
  1.5 0.6 %copy-done.1 = f32[4,1,2,128]{3,2,1,0:T(2,128)S(1)} copy-done((f32[4,1,2,128]{3,2,1,0:T(2,128)S(1)}, f32[4,1,2,128]{3,2,1,0:T(2,128)}, u32[]{:S(2)}) %copy-start.1) | copy-done | bytes 4120
  2.1 0.0 copy-start
  2.1 0.8 %copy-done = f32[4,1,32,128]{3,2,1,0:T(8,128)S(1)} copy-done((f32[4,1,32,128]{3,2,1,0:T(8,128)S(1)}, f32[4,1,32,128]{3,2,1,0:T(8,128)}, u32[]{:S(2)}) %copy-start) | copy-done | bytes 65560
  2.9 53.0 %window.1 = (f32[4,32,128]{2,1,0:T(8,128)S(1)}, f32[4,32,128]{2,1,0:T(8,128)S(1)}) custom-call(s32[4,5]{1,0:T(4,128)S(1)} %pad_add_fusion.slots_ref, f32[4,5]{1,0:T(4,128)S(1)} %pad_convert_fusion.masks_ref, f32[4,2,128]{2,1,0:T(2,128)S(1)} %bitcast.12, f32[4,32,128]{2,1,0:T(8,128)S(1)} %bitcast.9), custom_call_target="tpu_custom_call" | custom-call | tf_op jit(solution)/shard_map/window/pallas_call | solution.py:408
  56.0 0.6 %copy.9 = f32[4,1,32,128]{3,2,1,0:T(8,128)} copy(f32[4,1,32,128]{3,2,1,0:T(8,128)S(1)} %bitcast.11) | data formatting | bytes 131072
  56.6 0.6 %copy.10 = f32[4,1,32,128]{3,2,1,0:T(8,128)} copy(f32[4,1,32,128]{3,2,1,0:T(8,128)S(1)} %bitcast.10) | data formatting | bytes 131072
  (4 shorter events, 0.0 us)
Async XLA Ops:
  0.6 0.7 %copy-start.2 = (s32[4,1,4]{2,1,0:T(1,128)S(1)}, s32[4,1,4]{2,1,0:T(1,128)}, u32[]{:S(2)}) copy-start(s32[4,1,4]{2,1,0:T(1,128)} %param.5) | copy-start | bytes 196
  1.4 0.7 %copy-start.1 = (f32[4,1,2,128]{3,2,1,0:T(2,128)S(1)}, f32[4,1,2,128]{3,2,1,0:T(2,128)}, u32[]{:S(2)}) copy-start(f32[4,1,2,128]{3,2,1,0:T(2,128)} %param.3) | copy-start | bytes 12292
  2.1 0.8 %copy-start = (f32[4,1,32,128]{3,2,1,0:T(8,128)S(1)}, f32[4,1,32,128]{3,2,1,0:T(8,128)}, u32[]{:S(2)}) copy-start(f32[4,1,32,128]{3,2,1,0:T(8,128)} %param.4) | copy-start | bytes 196612
